TPU v7x, 256 devices: a whole 4x4x8 slice. The times are simulated.
256 devices in a mesh: feed: 32 (over z, x), tm: 8 (over y, core).
Axes of the slice: x: 4, y: 4, z: 8, core: 2. Of those that a mesh axis runs over, the one named last changes fastest.
Arguments:
- voltages: bfloat16 [2048, 262144], P('feed', 'tm'), may hold values from -6 to 6
- feed_slot: int32 [2048], replicated, may hold values from 0 to 2047, each once
- channel_flags: int32 [1024], replicated, may hold values from 0 to 1, as said below
Outputs:
- beam_power: float32 [768, 16, 1024], P(('feed', 'tm'))
Inputs may be any that keep to these rules, and one draw needn't show every extreme that they name: `channel_flags`: exactly 768 entries are 1. `feed_slot`: each slot is named by exactly one input.
All inputs are finite; a program needn't handle non-finite values.
Results may differ from a plain program's by a relative error of at most 0.01.
Values may be sent and summed in bfloat16 or wider, within the bound.
No kernel may reach another device: no remote copies, remote signals or barrier semaphores. Data moves between devices by JAX's collectives and lax.ppermute only.
A program may use at most 128 MiB of HBM per device.

v0:
```python
import math

import jax
import jax.numpy as jnp
import numpy as np
from jax import lax
from jax.experimental import pallas as pl
from jax.experimental.pallas import tpu as pltpu
from jax.sharding import PartitionSpec as P

CHANNELS = 1024
TAPS = 4
CYL = 4
NS = 256
UPCH = 16
FRAME = 2048
N_FEED = 32
N_TM = 8
IN_DEV = 64
FR_DEV = 16
LIVE_DEV = 3
LIVE = 768
EARLY = 4
MIB = 1 << 20


def window_table():
    length = TAPS * FRAME
    sample = np.arange(length, dtype=np.float64)
    offset = (sample - length / 2 + 0.5) / FRAME
    taper = 0.5 - 0.5 * np.cos(2.0 * np.pi * (sample + 0.5) / length)
    return (np.sinc(offset) * taper).reshape(TAPS, FRAME).astype(np.float32)


def cos_sin(modulus, first, second):
    product = np.arange(first)[:, None] * np.arange(second)[None, :] % modulus
    angle = product * (2.0 * np.pi / modulus)
    scale = 1.0 / math.sqrt(modulus)
    return np.cos(angle) * scale, np.sin(angle) * scale


def position_table():
    cosine, sine = cos_sin(NS, NS, NS)
    return np.concatenate([cosine, sine], axis=1)


def sub_channel_table():
    cosine, sine = cos_sin(UPCH, UPCH, UPCH)
    same = np.eye(N_TM)
    real = np.stack([cosine, sine])
    imag = np.stack([-sine, cosine])
    both = np.stack([real, imag])
    return np.einsum("qruk,ts->qtkurs", both, same).reshape(256, 256)


def unit_circle(phase):
    quadrant = (phase + 256) >> 9
    x = (phase - (quadrant << 9)).astype(jnp.float32) * np.float32(2.0 * np.pi / FRAME)
    x2 = x * x
    c = 1.0 + x2 * (-0.5 + x2 * (1.0 / 24 + x2 * (-1.0 / 720 + x2 * (1.0 / 40320))))
    s = x * (1.0 + x2 * (-1.0 / 6 + x2 * (1.0 / 120 + x2 * (-1.0 / 5040 + x2 * (1.0 / 362880)))))
    odd = (quadrant & 1) == 1
    cos_mag = jnp.where(odd, s, c)
    sin_mag = jnp.where(odd, c, s)
    cosine = jnp.where(((quadrant + 1) & 2) == 2, -cos_mag, cos_mag)
    sine = jnp.where((quadrant & 2) == 2, -sin_mag, sin_mag)
    return cosine, sine


def filter_block(window_ref, load, store, frames, lane):
    taps = [window_ref[pl.ds(t, 1), pl.ds(lane, 128)] for t in range(TAPS)]
    for rows in range(0, IN_DEV, 16):
        held = {}
        for f in frames:
            total = None
            for t in range(TAPS):
                g = f - TAPS + 1 + t
                if g not in held:
                    held[g] = load(g, rows).astype(jnp.float32)
                term = taps[t] * held[g]
                total = term if total is None else total + term
            store(f, rows, total.astype(jnp.bfloat16))


def first_kernel(flags_ref, volt_ref, window_ref, table_ref, late_ref, cos_ref, sin_ref, dcos_ref, dsin_ref):
    rows = lax.broadcasted_iota(jnp.int32, (CHANNELS, CHANNELS), 0)
    cols = lax.broadcasted_iota(jnp.int32, (CHANNELS, CHANNELS), 1)
    upto = (rows <= cols).astype(jnp.float32).astype(jnp.bfloat16)
    flags = jnp.broadcast_to(flags_ref[...].astype(jnp.float32), (16, CHANNELS)).astype(jnp.bfloat16)
    count = jnp.dot(flags, upto, preferred_element_type=jnp.float32)[0:1].astype(jnp.int32)
    ones = jnp.ones((CHANNELS, 128), jnp.bfloat16)

    def place(step, carry):
        row = lax.broadcasted_iota(jnp.int32, (64, CHANNELS), 0) + step * 64
        chunk, owner, t = row >> 8, (row >> 3) & 31, row & 7
        rank = owner * (LIVE_DEV * N_TM) + t * LIVE_DEV + chunk
        below = (count <= rank).astype(jnp.float32).astype(jnp.bfloat16)
        channel = jnp.dot(below, ones, preferred_element_type=jnp.float32).astype(jnp.int32)
        at = pl.ds(pl.multiple_of(step * 64, 64), 64)
        lane = lax.broadcasted_iota(jnp.int32, (64, 128), 1)
        c, s = unit_circle((channel * lane) & (FRAME - 1))
        scale = np.float32(1.0 / math.sqrt(FRAME))
        cos_ref[at, :] = c * scale
        sin_ref[at, :] = s * scale
        c, s = unit_circle((channel * 128) & (FRAME - 1))
        dcos_ref[at, :] = c
        dsin_ref[at, :] = s
        return carry

    lax.fori_loop(0, LIVE // 64, place, 0)

    def turn(step, carry):
        at = pl.ds(pl.multiple_of(step * 64, 64), 64)
        c, s = cos_ref[at, :].reshape(8, 8, 128), sin_ref[at, :].reshape(8, 8, 128)
        dc, ds = dcos_ref[at, :].reshape(8, 8, 128), dsin_ref[at, :].reshape(8, 8, 128)
        out = pl.ds(pl.multiple_of(step * 128, 128), 128)
        for v in range(FRAME // 128):
            pair = jnp.stack([c, -s], axis=1).reshape(128, 128)
            table_ref[out, v * 128 : (v + 1) * 128] = pair.astype(jnp.bfloat16)
            if v < FRAME // 128 - 1:
                c, s = dc * c - ds * s, ds * c + dc * s
        return carry

    lax.fori_loop(0, LIVE // 64, turn, 0)

    def lanes(b, carry):
        lane = pl.multiple_of(b * 128, 128)

        def load(f, rows):
            return volt_ref[rows : rows + 16, pl.ds(pl.multiple_of(f * FRAME + lane, 128), 128)]

        def store(f, rows, value):
            at = (f - EARLY) * IN_DEV + rows
            late_ref[at : at + 16, pl.ds(lane, 128)] = value

        filter_block(window_ref, load, store, range(EARLY, FR_DEV), lane)
        return carry

    lax.fori_loop(0, FRAME // 128, lanes, 0)


def transposed_dot(a, b):
    return lax.dot_general(a, b, (((1,), (1,)), ((), ())), preferred_element_type=jnp.float32)


def spectra_into(table, early_ref, late_ref, out_ref):
    for n in range(FR_DEV * IN_DEV // 256):
        block = early_ref[...] if n == 0 else late_ref[(n - 1) * 256 : n * 256, :]
        out_ref[:, n * 256 : (n + 1) * 256] = transposed_dot(table, block).astype(jnp.bfloat16)


def second_kernel(halo_ref, volt_ref, window_ref, table_ref, late_ref, early_ref, out_ref):
    def lanes(b, carry):
        lane = pl.multiple_of(b * 128, 128)

        def load(f, rows):
            ref, g = (halo_ref, f + TAPS - 1) if f < 0 else (volt_ref, f)
            return ref[rows : rows + 16, pl.ds(pl.multiple_of(g * FRAME + lane, 128), 128)]

        def store(f, rows, value):
            at = f * IN_DEV + rows
            early_ref[at : at + 16, pl.ds(lane, 128)] = value

        filter_block(window_ref, load, store, range(EARLY), lane)
        return carry

    lax.fori_loop(0, FRAME // 128, lanes, 0)
    spectra_into(table_ref[...], early_ref, late_ref, out_ref)


def later_kernel(table_ref, early_ref, late_ref, out_ref):
    spectra_into(table_ref[...], early_ref, late_ref, out_ref)


def beam_kernel(recv_ref, place_ref, position_ref, sub_ref, out_ref, x_ref, part_ref, beam_ref, power_ref):
    p = pl.program_id(0)

    @pl.when(p == 0)
    def _():
        low = lax.broadcasted_iota(jnp.int32, (16, 128), 1) < IN_DEV

        def pairs(s, carry):
            lane = pl.multiple_of(s * 128, 128)
            for g in range(FR_DEV // 2):
                a = recv_ref[2 * s, :, g * 128 : (g + 1) * 128].astype(jnp.float32)
                b = recv_ref[2 * s + 1, :, g * 128 : (g + 1) * 128].astype(jnp.float32)
                even = jnp.where(low, a, pltpu.roll(b, 64, 1))
                odd = jnp.where(low, pltpu.roll(a, 64, 1), b)
                x_ref[g * 32 : g * 32 + 16, pl.ds(lane, 128)] = even.astype(jnp.bfloat16)
                x_ref[g * 32 + 16 : g * 32 + 32, pl.ds(lane, 128)] = odd.astype(jnp.bfloat16)
            return carry

        lax.fori_loop(0, N_FEED // 2, pairs, 0)

    for y in range(CYL):
        cells = jnp.dot(
            x_ref[...], place_ref[:, y * NS : (y + 1) * NS], preferred_element_type=jnp.float32
        ).astype(jnp.bfloat16)
        both = jnp.dot(cells, position_ref[...], preferred_element_type=jnp.float32)
        both = both.reshape(FR_DEV, 2, N_TM, 2 * NS)
        part_ref[y, :, 0] = both[:, 0, :, :NS] + both[:, 1, :, NS:]
        part_ref[y, :, 1] = both[:, 1, :, :NS] - both[:, 0, :, NS:]

    def join(f, carry):
        re = [part_ref[y, f, 0] for y in range(CYL)]
        im = [part_ref[y, f, 1] for y in range(CYL)]
        re_s, re_d = re[0] + re[2], re[0] - re[2]
        im_s, im_d = im[0] + im[2], im[0] - im[2]
        re_t, re_e = re[1] + re[3], re[1] - re[3]
        im_t, im_e = im[1] + im[3], im[1] - im[3]
        out_re = [re_s + re_t, re_d + im_e, re_s - re_t, re_d - im_e]
        out_im = [im_s + im_t, im_d - re_e, im_s - im_t, im_d + re_e]
        at = pl.ds(pl.multiple_of(f * 16, 16), 16)
        for e in range(CYL):
            value = jnp.concatenate([out_re[e], out_im[e]], axis=0) * 0.5
            beam_ref[at, e * NS : (e + 1) * NS] = value.astype(jnp.bfloat16)
        return carry

    lax.fori_loop(0, FR_DEV, join, 0)

    for e in range(CYL):
        at = slice(e * NS, (e + 1) * NS)
        up = jnp.dot(sub_ref[...], beam_ref[:, at], preferred_element_type=jnp.float32)
        power = up[:128] * up[:128] + up[128:] * up[128:]

        @pl.when(p == 0)
        def _():
            power_ref[:, at] = power

        @pl.when(p == 1)
        def _():
            out_ref[:, at] = (power_ref[:, at] + power).astype(jnp.bfloat16)


def cost(flops, nbytes):
    return pl.CostEstimate(flops=int(flops), bytes_accessed=int(nbytes), transcendentals=0)


def whole(shape, *index):
    index = index or (0,) * len(shape)
    return pl.BlockSpec(shape, lambda *_: index)


def local(voltages, feed_slot, channel_flags):
    bf16, f32 = jnp.bfloat16, jnp.float32
    history = voltages[:, (FR_DEV - TAPS + 1) * FRAME :]
    halo = lax.ppermute(history, "tm", [(i, i + 1) for i in range(N_TM - 1)])
    window = jnp.asarray(window_table())
    rows = FR_DEV * IN_DEV
    early_rows = EARLY * IN_DEV
    table, late = pl.pallas_call(
        first_kernel,
        name="table_and_filter",
        out_shape=[
            jax.ShapeDtypeStruct((2 * LIVE, FRAME), bf16),
            jax.ShapeDtypeStruct((rows - early_rows, FRAME), bf16),
        ],
        scratch_shapes=[pltpu.VMEM((LIVE, 128), f32)] * 4,
        compiler_params=pltpu.CompilerParams(vmem_limit_bytes=32 * MIB),
        cost_estimate=cost(9e9, 13 * MIB),
    )(channel_flags.reshape(1, CHANNELS), voltages, window)
    params = pltpu.CompilerParams(vmem_limit_bytes=32 * MIB)
    chunk_rows = 2 * LIVE // LIVE_DEV
    early, sent = pl.pallas_call(
        second_kernel,
        name="filter_and_spectra",
        grid=(1,),
        in_specs=[
            whole((IN_DEV, (TAPS - 1) * FRAME)),
            whole((IN_DEV, EARLY * FRAME)),
            whole((TAPS, FRAME)),
            whole((chunk_rows, FRAME)),
            whole((rows - early_rows, FRAME)),
        ],
        out_specs=[whole((early_rows, FRAME)), whole((chunk_rows, rows))],
        out_shape=[
            jax.ShapeDtypeStruct((early_rows, FRAME), bf16),
            jax.ShapeDtypeStruct((chunk_rows, rows), bf16),
        ],
        compiler_params=params,
        cost_estimate=cost(2.5e9, 8 * MIB),
    )(halo, voltages, window, table, late)
    chunks = [sent]
    for i in range(1, LIVE_DEV):
        chunks.append(
            pl.pallas_call(
                later_kernel,
                name="spectra",
                grid=(1,),
                in_specs=[
                    whole((chunk_rows, FRAME), i, 0),
                    whole((early_rows, FRAME)),
                    whole((rows - early_rows, FRAME)),
                ],
                out_specs=whole((chunk_rows, rows)),
                out_shape=jax.ShapeDtypeStruct((chunk_rows, rows), bf16),
                compiler_params=params,
                cost_estimate=cost(2.2e9, 8 * MIB),
            )(table, early, late)
        )
    inputs = N_FEED * IN_DEV
    place = (feed_slot[:, None] == jnp.arange(inputs, dtype=jnp.int32)[None, :]).astype(bf16)
    position = jnp.asarray(position_table(), dtype=bf16)
    sub = jnp.asarray(sub_channel_table(), dtype=bf16)
    powers = []
    for chunk in chunks:
        got = lax.all_to_all(
            chunk.reshape(N_FEED, 16, rows), "feed", split_axis=0, concat_axis=0, tiled=True
        )
        power = pl.pallas_call(
            beam_kernel,
            name="beams_and_power",
            grid=(2,),
            in_specs=[
                whole((N_FEED, 16, rows)),
                pl.BlockSpec((inputs, CYL * NS), lambda p: (0, p)),
                whole((NS, 2 * NS)),
                whole((256, 256)),
            ],
            out_specs=whole((128, CYL * NS)),
            out_shape=jax.ShapeDtypeStruct((128, CYL * NS), bf16),
            scratch_shapes=[
                pltpu.VMEM((256, inputs), bf16),
                pltpu.VMEM((CYL, FR_DEV, 2, N_TM, NS), f32),
                pltpu.VMEM((256, CYL * NS), bf16),
                pltpu.VMEM((128, CYL * NS), f32),
            ],
            compiler_params=pltpu.CompilerParams(vmem_limit_bytes=32 * MIB),
            cost_estimate=cost(3e9, 10 * MIB),
        )(got, place, position, sub)
        shared = lax.all_to_all(
            power.reshape(N_TM, UPCH, CYL * NS), "tm", split_axis=0, concat_axis=0, tiled=True
        )
        powers.append(shared)
    scale = 1.0 / (2.0 * N_TM * (FR_DEV // UPCH))
    return jnp.stack([jnp.sum(x.astype(f32), axis=0) * scale for x in powers])


def solution(mesh):
    in_specs = (P("feed", "tm"), P(), P())
    out_specs = P(("feed", "tm"), None, None)
    return jax.shard_map(local, mesh=mesh, in_specs=in_specs, out_specs=out_specs, check_vma=False)
```

profile of v0, /device:TPU:1, one launch (start us, length us, event | category | flops | bytes accessed | tf_op | source)
XLA Modules:
  0.0 172.1 jit_solution(2972937094225623410)
XLA Ops:
  1.2 4.6 %collective-permute-start = (bf16[64,6144]{1,0:T(8,128)(2,1)S(1)}, bf16[64,6144]{1,0:T(8,128)(2,1)S(1)}, u32[]{:S(2)}, u32[]{:S(2)}) collective-permute-start(bf16[64,6144]{1,0:T(8,128)(2,1)S(1)} %slice.3), channel_id=1, source_target_pairs={{0,1},{1,2},{2,3},{3,4},{4,5},{5,6},{6,7},{8,9},{9,10},{10,11},{11... | collective-permute-start | bytes 2359304 | tf_op jit(solution)/shard_map/ppermute | solution.py:247
  5.8 2.2 %copy-done.5 = bf16[64,32768]{1,0:T(8,128)(2,1)S(1)} copy-done((bf16[64,32768]{1,0:T(8,128)(2,1)S(1)}, bf16[64,32768]{1,0:T(8,128)(2,1)}, u32[]{:S(2)}) %copy-start.5) | copy-done | bytes 4194328
  9.4 7.3 %table_and_filter.1 = (bf16[1536,2048]{1,0:T(8,128)(2,1)S(1)}, bf16[768,2048]{1,0:T(8,128)(2,1)S(1)}) custom-call(s32[1,1024]{1,0:T(1,128)S(1)} %bitcast.16, bf16[64,32768]{1,0:T(8,128)(2,1)S(1)} %copy-done.5, f32[4,2048]{1,0:T(4,128)S(1)} %copy-done.13), custom_call_target="tpu_custom_call" | custom-call | flops 8999999488 | bytes 13631488 | tf_op jit(solution)/shard_map/table_and_filter/pallas_call | solution.py:251
  16.8 3.2 %filter_and_spectra.1 = (bf16[256,2048]{1,0:T(8,128)(2,1)S(1)}, bf16[512,1024]{1,0:T(8,128)(2,1)S(1)}) custom-call(bf16[64,6144]{1,0:T(8,128)(2,1)S(1)} %collective-permute-done.halo_ref, bf16[64,32768]{1,0:T(8,128)(2,1)S(1)} %copy-done.6, f32[4,2048]{1,0:T(4,128)S(1)} %copy-done.13, bf16[1536,2048]{1,0:T(8,128)(2,1)S(1)} %get-tuple-element.9.table_ref, ...), custom_call_target="tpu_custom_call" | custom-call | flops 2500000000 | bytes 8388608 | tf_op jit(solution)/shard_map/filter_and_spectra/pallas_call | solution.py:264
  20.0 2.7 %copy-done = bf16[1536,2048]{1,0:T(8,128)(2,1)} copy-done((bf16[1536,2048]{1,0:T(8,128)(2,1)}, bf16[1536,2048]{1,0:T(8,128)(2,1)S(1)}, u32[]{:S(2)}) %copy-start) | copy-done | bytes 6291480
  24.6 11.2 %all-to-all-start = ((bf16[32,16,1024]{2,1,0:T(8,128)(2,1)}), bf16[32,16,1024]{2,1,0:T(8,128)(2,1)}, u32[]{:S(2)}, u32[]{:S(2)}) async-start(bf16[32,16,1024]{2,1,0:T(8,128)(2,1)} %bitcast.15), calls=%async_computation | async-start | bytes 2097152 | tf_op jit(solution)/shard_map/all_to_all | solution.py:307
  35.8 2.8 %copy-done.1 = bf16[1536,2048]{1,0:T(8,128)(2,1)S(1)} copy-done((bf16[1536,2048]{1,0:T(8,128)(2,1)S(1)}, bf16[1536,2048]{1,0:T(8,128)(2,1)}, u32[]{:S(2)}) %copy-start.1) | copy-done | bytes 6291480
  39.8 2.4 %spectra.3 = bf16[512,1024]{1,0:T(8,128)(2,1)S(1)} custom-call(bf16[1536,2048]{1,0:T(8,128)(2,1)S(1)} %copy-done.1, bf16[256,2048]{1,0:T(8,128)(2,1)S(1)} %copy-done.10, bf16[768,2048]{1,0:T(8,128)(2,1)S(1)} %get-tuple-element.10.late_ref), custom_call_target="tpu_custom_call" | custom-call | flops 2200000000 | bytes 8388608 | tf_op jit(solution)/shard_map/spectra/pallas_call | solution.py:286
  43.2 20.0 %all-to-all-done.recv_ref = bf16[32,16,1024]{2,1,0:T(8,128)(2,1)} async-done(((bf16[32,16,1024]{2,1,0:T(8,128)(2,1)}), bf16[32,16,1024]{2,1,0:T(8,128)(2,1)}, u32[]{:S(2)}, u32[]{:S(2)}) %all-to-all-start) | async-done | bytes 1048608 | tf_op jit(solution)/shard_map/all_to_all | solution.py:307
  63.3 5.7 %all-to-all-start.4 = ((bf16[32,16,1024]{2,1,0:T(8,128)(2,1)}), bf16[32,16,1024]{2,1,0:T(8,128)(2,1)}, u32[]{:S(2)}, u32[]{:S(2)}) async-start(bf16[32,16,1024]{2,1,0:T(8,128)(2,1)} %bitcast.14), calls=%async_computation.4 | async-start | bytes 2097152 | tf_op jit(solution)/shard_map/all_to_all | solution.py:307
  69.0 2.8 %copy-done.2 = bf16[1536,2048]{1,0:T(8,128)(2,1)S(1)} copy-done((bf16[1536,2048]{1,0:T(8,128)(2,1)S(1)}, bf16[1536,2048]{1,0:T(8,128)(2,1)}, u32[]{:S(2)}) %copy-start.2) | copy-done | bytes 6291480
  73.0 2.4 %spectra.2 = bf16[512,1024]{1,0:T(8,128)(2,1)S(1)} custom-call(bf16[1536,2048]{1,0:T(8,128)(2,1)S(1)} %copy-done.2, bf16[256,2048]{1,0:T(8,128)(2,1)S(1)} %copy-done.11, bf16[768,2048]{1,0:T(8,128)(2,1)S(1)} %get-tuple-element.10.late_ref), custom_call_target="tpu_custom_call" | custom-call | flops 2200000000 | bytes 8388608 | tf_op jit(solution)/shard_map/spectra/pallas_call | solution.py:286
  76.3 20.7 %all-to-all-done.4.recv_ref = bf16[32,16,1024]{2,1,0:T(8,128)(2,1)} async-done(((bf16[32,16,1024]{2,1,0:T(8,128)(2,1)}), bf16[32,16,1024]{2,1,0:T(8,128)(2,1)}, u32[]{:S(2)}, u32[]{:S(2)}) %all-to-all-start.4) | async-done | bytes 1048608 | tf_op jit(solution)/shard_map/all_to_all | solution.py:307
  97.0 5.2 %all-to-all-start.2 = ((bf16[32,16,1024]{2,1,0:T(8,128)(2,1)}), bf16[32,16,1024]{2,1,0:T(8,128)(2,1)S(1)}, u32[]{:S(2)}, u32[]{:S(2)}) async-start(bf16[32,16,1024]{2,1,0:T(8,128)(2,1)} %bitcast.13), calls=%async_computation.2 | async-start | bytes 2097152 | tf_op jit(solution)/shard_map/all_to_all | solution.py:307
  102.2 1.4 fusion.place_ref
  103.7 12.8 %beams_and_power.3 = bf16[128,1024]{1,0:T(8,128)(2,1)} custom-call(bf16[32,16,1024]{2,1,0:T(8,128)(2,1)} %all-to-all-done.recv_ref, bf16[2048,2048]{1,0:T(8,128)(2,1)S(1)} %fusion.place_ref, bf16[256,512]{1,0:T(8,128)(2,1)S(1)} %copy-done.15, bf16[256,256]{1,0:T(8,128)(2,1)S(1)} %copy-done.16), custom_call_target="tpu_custom_call" | custom-call | flops 3000000000 | bytes 10485760 | tf_op jit(solution)/shard_map/beams_and_power/pallas_call | solution.py:310
  116.5 12.0 %beams_and_power.5 = bf16[128,1024]{1,0:T(8,128)(2,1)} custom-call(bf16[32,16,1024]{2,1,0:T(8,128)(2,1)} %all-to-all-done.4.recv_ref, bf16[2048,2048]{1,0:T(8,128)(2,1)S(1)} %fusion.place_ref, bf16[256,512]{1,0:T(8,128)(2,1)S(1)} %copy-done.15, bf16[256,256]{1,0:T(8,128)(2,1)S(1)} %copy-done.16), custom_call_target="tpu_custom_call" | custom-call | flops 3000000000 | bytes 10485760 | tf_op jit(solution)/shard_map/beams_and_power/pallas_call | solution.py:310
  128.5 6.1 %all-to-all-start.1 = ((bf16[8,16,1024]{2,1,0:T(8,128)(2,1)}), bf16[8,16,1024]{2,1,0:T(8,128)(2,1)S(1)}, u32[]{:S(2)}, u32[]{:S(2)}) async-start(bf16[8,16,1024]{2,1,0:T(8,128)(2,1)} %bitcast.2), calls=%async_computation.1 | async-start | bytes 524288 | tf_op jit(solution)/shard_map/all_to_all | solution.py:331
  134.7 3.4 %copy-done.4 = bf16[2048,2048]{1,0:T(8,128)(2,1)S(1)} copy-done((bf16[2048,2048]{1,0:T(8,128)(2,1)S(1)}, bf16[2048,2048]{1,0:T(8,128)(2,1)}, u32[]{:S(2)}) %copy-start.4) | copy-done | bytes 8388632
  138.0 11.1 %beams_and_power.4 = bf16[128,1024]{1,0:T(8,128)(2,1)} custom-call(bf16[32,16,1024]{2,1,0:T(8,128)(2,1)S(1)} %all-to-all-done.2.recv_ref, bf16[2048,2048]{1,0:T(8,128)(2,1)S(1)} %copy-done.4, bf16[256,512]{1,0:T(8,128)(2,1)S(1)} %copy-done.15, bf16[256,256]{1,0:T(8,128)(2,1)S(1)} %copy-done.16), custom_call_target="tpu_custom_call" | custom-call | flops 3000000000 | bytes 10485760 | tf_op jit(solution)/shard_map/beams_and_power/pallas_call | solution.py:310
  149.1 4.8 %all-to-all-start.5 = ((bf16[8,16,1024]{2,1,0:T(8,128)(2,1)}), bf16[8,16,1024]{2,1,0:T(8,128)(2,1)S(1)}, u32[]{:S(2)}, u32[]{:S(2)}) async-start(bf16[8,16,1024]{2,1,0:T(8,128)(2,1)} %bitcast.8), calls=%async_computation.5 | async-start | bytes 524288 | tf_op jit(solution)/shard_map/all_to_all | solution.py:331
  154.0 6.4 %all-to-all-done.5 = bf16[8,16,1024]{2,1,0:T(8,128)(2,1)S(1)} async-done(((bf16[8,16,1024]{2,1,0:T(8,128)(2,1)}), bf16[8,16,1024]{2,1,0:T(8,128)(2,1)S(1)}, u32[]{:S(2)}, u32[]{:S(2)}) %all-to-all-start.5) | async-done | bytes 262176 | tf_op jit(solution)/shard_map/all_to_all | solution.py:331
  160.5 4.4 %all-to-all-start.3 = ((bf16[8,16,1024]{2,1,0:T(8,128)(2,1)}), bf16[8,16,1024]{2,1,0:T(8,128)(2,1)S(1)}, u32[]{:S(2)}, u32[]{:S(2)}) async-start(bf16[8,16,1024]{2,1,0:T(8,128)(2,1)} %bitcast.5), calls=%async_computation.3 | async-start | bytes 524288 | tf_op jit(solution)/shard_map/all_to_all | solution.py:331
  164.9 6.5 %all-to-all-done.3 = bf16[8,16,1024]{2,1,0:T(8,128)(2,1)S(1)} async-done(((bf16[8,16,1024]{2,1,0:T(8,128)(2,1)}), bf16[8,16,1024]{2,1,0:T(8,128)(2,1)S(1)}, u32[]{:S(2)}, u32[]{:S(2)}) %all-to-all-start.3) | async-done | bytes 262176 | tf_op jit(solution)/shard_map/all_to_all | solution.py:331
  (42 shorter events, 9.9 us)
Async XLA Ops:
  1.2 15.6 %collective-permute-start = (bf16[64,6144]{1,0:T(8,128)(2,1)S(1)}, bf16[64,6144]{1,0:T(8,128)(2,1)S(1)}, u32[]{:S(2)}, u32[]{:S(2)}) collective-permute-start(bf16[64,6144]{1,0:T(8,128)(2,1)S(1)} %slice.3), channel_id=1, source_target_pairs={{0,1},{1,2},{2,3},{3,4},{4,5},{5,6},{6,7},{8,9},{9,10},{10,11},{11... | collective-permute-start | bytes 2359304 | tf_op jit(solution)/shard_map/ppermute | solution.py:247
  5.8 2.2 %copy-start.5 = (bf16[64,32768]{1,0:T(8,128)(2,1)S(1)}, bf16[64,32768]{1,0:T(8,128)(2,1)}, u32[]{:S(2)}) copy-start(bf16[64,32768]{1,0:T(8,128)(2,1)} %volt_ref.3) | copy-start | bytes 12582916
  8.0 0.8 copy-start.13
  9.4 7.3 %copy-start.6 = (bf16[64,32768]{1,0:T(8,128)(2,1)S(1)}, bf16[64,32768]{1,0:T(8,128)(2,1)}, u32[]{:S(2)}) copy-start(bf16[64,32768]{1,0:T(8,128)(2,1)} %volt_ref.3) | copy-start | bytes 12582916
  20.0 2.7 %copy-start = (bf16[1536,2048]{1,0:T(8,128)(2,1)}, bf16[1536,2048]{1,0:T(8,128)(2,1)S(1)}, u32[]{:S(2)}) copy-start(bf16[1536,2048]{1,0:T(8,128)(2,1)S(1)} %get-tuple-element.9.table_ref) | copy-start | bytes 18874372
  22.7 1.0 copy-start.9
  23.6 1.0 copy-start.12
  24.6 38.6 %all-to-all-start = ((bf16[32,16,1024]{2,1,0:T(8,128)(2,1)}), bf16[32,16,1024]{2,1,0:T(8,128)(2,1)}, u32[]{:S(2)}, u32[]{:S(2)}) async-start(bf16[32,16,1024]{2,1,0:T(8,128)(2,1)} %bitcast.15), calls=%async_computation | async-start | bytes 2097152 | tf_op jit(solution)/shard_map/all_to_all | solution.py:307
  35.8 2.8 %copy-start.1 = (bf16[1536,2048]{1,0:T(8,128)(2,1)S(1)}, bf16[1536,2048]{1,0:T(8,128)(2,1)}, u32[]{:S(2)}) copy-start(bf16[1536,2048]{1,0:T(8,128)(2,1)} %copy-done) | copy-start | bytes 18874372
  38.6 1.2 copy-start.10
  42.2 1.1 copy-start.8
  43.2 59.0 %copy-start.17 = (s32[2048]{0:T(1024)S(1)}, s32[2048]{0:T(1024)}, u32[]{:S(2)}) copy-start(s32[2048]{0:T(1024)} %param.7) | copy-start | bytes 24580
  63.3 33.7 %all-to-all-start.4 = ((bf16[32,16,1024]{2,1,0:T(8,128)(2,1)}), bf16[32,16,1024]{2,1,0:T(8,128)(2,1)}, u32[]{:S(2)}, u32[]{:S(2)}) async-start(bf16[32,16,1024]{2,1,0:T(8,128)(2,1)} %bitcast.14), calls=%async_computation.4 | async-start | bytes 2097152 | tf_op jit(solution)/shard_map/all_to_all | solution.py:307
  69.0 2.8 %copy-start.2 = (bf16[1536,2048]{1,0:T(8,128)(2,1)S(1)}, bf16[1536,2048]{1,0:T(8,128)(2,1)}, u32[]{:S(2)}) copy-start(bf16[1536,2048]{1,0:T(8,128)(2,1)} %copy-done) | copy-start | bytes 18874372
  71.8 1.2 copy-start.11
  73.0 30.6 %copy-start.15 = (bf16[256,512]{1,0:T(8,128)(2,1)S(1)}, bf16[256,512]{1,0:T(8,128)(2,1)}, u32[]{:S(2)}) copy-start(bf16[256,512]{1,0:T(8,128)(2,1)} %constant.11.clone.position_ref) | copy-start | bytes 786436
  73.0 30.6 %copy-start.16 = (bf16[256,256]{1,0:T(8,128)(2,1)S(1)}, bf16[256,256]{1,0:T(8,128)(2,1)}, u32[]{:S(2)}) copy-start(bf16[256,256]{1,0:T(8,128)(2,1)} %constant.12.clone.sub_ref) | copy-start | bytes 393220
  75.4 1.0 copy-start.7
  97.0 31.5 %all-to-all-start.2 = ((bf16[32,16,1024]{2,1,0:T(8,128)(2,1)}), bf16[32,16,1024]{2,1,0:T(8,128)(2,1)S(1)}, u32[]{:S(2)}, u32[]{:S(2)}) async-start(bf16[32,16,1024]{2,1,0:T(8,128)(2,1)} %bitcast.13), calls=%async_computation.2 | async-start | bytes 2097152 | tf_op jit(solution)/shard_map/all_to_all | solution.py:307
  103.6 12.8 %copy-start.3 = (bf16[2048,2048]{1,0:T(8,128)(2,1)}, bf16[2048,2048]{1,0:T(8,128)(2,1)S(1)}, u32[]{:S(2)}) copy-start(bf16[2048,2048]{1,0:T(8,128)(2,1)S(1)} %fusion.place_ref) | copy-start | bytes 25165828
  128.5 20.6 %all-to-all-start.1 = ((bf16[8,16,1024]{2,1,0:T(8,128)(2,1)}), bf16[8,16,1024]{2,1,0:T(8,128)(2,1)S(1)}, u32[]{:S(2)}, u32[]{:S(2)}) async-start(bf16[8,16,1024]{2,1,0:T(8,128)(2,1)} %bitcast.2), calls=%async_computation.1 | async-start | bytes 524288 | tf_op jit(solution)/shard_map/all_to_all | solution.py:331
  134.7 3.4 %copy-start.4 = (bf16[2048,2048]{1,0:T(8,128)(2,1)S(1)}, bf16[2048,2048]{1,0:T(8,128)(2,1)}, u32[]{:S(2)}) copy-start(bf16[2048,2048]{1,0:T(8,128)(2,1)} %copy-done.3) | copy-start | bytes 25165828
  149.1 11.3 %all-to-all-start.5 = ((bf16[8,16,1024]{2,1,0:T(8,128)(2,1)}), bf16[8,16,1024]{2,1,0:T(8,128)(2,1)S(1)}, u32[]{:S(2)}, u32[]{:S(2)}) async-start(bf16[8,16,1024]{2,1,0:T(8,128)(2,1)} %bitcast.8), calls=%async_computation.5 | async-start | bytes 524288 | tf_op jit(solution)/shard_map/all_to_all | solution.py:331
  160.5 10.9 %all-to-all-start.3 = ((bf16[8,16,1024]{2,1,0:T(8,128)(2,1)}), bf16[8,16,1024]{2,1,0:T(8,128)(2,1)S(1)}, u32[]{:S(2)}, u32[]{:S(2)}) async-start(bf16[8,16,1024]{2,1,0:T(8,128)(2,1)} %bitcast.5), calls=%async_computation.3 | async-start | bytes 524288 | tf_op jit(solution)/shard_map/all_to_all | solution.py:331
  (1 other events, 0.7 us)
where the time goes:
time: 173 us; the launch traced here: 172 us
  waiting for transfers between devices  53.6 us (31%)
  Pallas kernels  51.2 us (30%)
  starting transfers between devices  42 us (24%)
  local copies, waits for them, and re-layouts  22.9 us (13%)
  other arithmetic  2.24 us (1%)
    all_to_all x3, waiting for transfers between devices, local(): lax.all_to_all(chunk.reshape(N_FEED, 16, rows), 'feed', split_axis=0, con...  40.7 us
    pallas_call x3, Pallas kernels, local(): pl.pallas_call(beam_kernel, name='beams_and_power', grid=(2,), in_specs=[...  36 us
    all_to_all x3, starting transfers between devices, local(): lax.all_to_all(chunk.reshape(N_FEED, 16, rows), 'feed', split_axis=0, con...  22.1 us
    unnamed x36, local copies, waits for them, and re-layouts  21.7 us
    all_to_all x3, starting transfers between devices, local(): lax.all_to_all(power.reshape(N_TM, UPCH, CYL * NS), 'tm', split_axis=0, c...  15.3 us
    all_to_all x3, waiting for transfers between devices, local(): lax.all_to_all(power.reshape(N_TM, UPCH, CYL * NS), 'tm', split_axis=0, c...  12.9 us
    pallas_call x1, Pallas kernels, local(): pl.pallas_call(first_kernel, name='table_and_filter', out_shape=[jax.Shap...  7.31 us
    pallas_call x2, Pallas kernels, local(): pl.pallas_call(later_kernel, name='spectra', grid=(1,), in_specs=[whole((...  4.72 us
  transfers between devices with their start and end apart: 7, of which 4 were waited for; matrix products, arithmetic and copies ran while one was open for 1% of the time, Pallas kernels for 28%

commit v1 on v0

v1 whole, which is shorter than its diff:
```python
import math

import jax
import jax.numpy as jnp
import numpy as np
from jax import lax
from jax.experimental import pallas as pl
from jax.experimental.pallas import tpu as pltpu
from jax.sharding import PartitionSpec as P

CHANNELS = 1024
TAPS = 4
CYL = 4
NS = 256
UPCH = 16
FRAME = 2048
N_FEED = 32
N_TM = 8
IN_DEV = 64
FR_DEV = 16
LIVE_DEV = 3
LIVE = 768
OWNERS = 256
PAIRS = FR_DEV // 2
EARLY = 4
MIB = 1 << 20


def window_table():
    length = TAPS * FRAME
    sample = np.arange(length, dtype=np.float64)
    offset = (sample - length / 2 + 0.5) / FRAME
    taper = 0.5 - 0.5 * np.cos(2.0 * np.pi * (sample + 0.5) / length)
    return (np.sinc(offset) * taper).reshape(TAPS, FRAME).astype(np.float32)


def cos_sin(modulus, first, second):
    product = np.arange(first)[:, None] * np.arange(second)[None, :] % modulus
    angle = product * (2.0 * np.pi / modulus)
    scale = 1.0 / math.sqrt(modulus)
    return np.cos(angle) * scale, np.sin(angle) * scale


def position_table():
    cosine, sine = cos_sin(NS, NS, NS)
    return np.concatenate([cosine, sine], axis=1)


def sub_channel_table():
    cosine, sine = cos_sin(UPCH, UPCH, UPCH)
    real = np.stack([cosine, sine])
    imag = np.stack([-sine, cosine])
    both = np.stack([real, imag]).reshape(2, 2, PAIRS, 2, UPCH)
    return np.einsum("qrghk,bd->qbkdhrg", both, np.eye(N_TM)).reshape(256, 256)


def unit_circle(phase):
    quadrant = (phase + 256) >> 9
    x = (phase - (quadrant << 9)).astype(jnp.float32) * np.float32(2.0 * np.pi / FRAME)
    x2 = x * x
    c = 1.0 + x2 * (-0.5 + x2 * (1.0 / 24 + x2 * (-1.0 / 720 + x2 * (1.0 / 40320))))
    s = x * (1.0 + x2 * (-1.0 / 6 + x2 * (1.0 / 120 + x2 * (-1.0 / 5040 + x2 * (1.0 / 362880)))))
    odd = (quadrant & 1) == 1
    cos_mag = jnp.where(odd, s, c)
    sin_mag = jnp.where(odd, c, s)
    cosine = jnp.where(((quadrant + 1) & 2) == 2, -cos_mag, cos_mag)
    sine = jnp.where((quadrant & 2) == 2, -sin_mag, sin_mag)
    return cosine, sine


def filter_block(window_ref, load, store, frames, lane):
    taps = [window_ref[pl.ds(t, 1), pl.ds(lane, 128)] for t in range(TAPS)]
    for rows in range(0, IN_DEV, 16):
        held = {}
        for f in frames:
            total = None
            for t in range(TAPS):
                g = f - TAPS + 1 + t
                if g not in held:
                    held[g] = load(g, rows).astype(jnp.float32)
                term = taps[t] * held[g]
                total = term if total is None else total + term
            store(f, rows, total.astype(jnp.bfloat16))


def table_kernel(flags_ref, table_ref, cos_ref, sin_ref, dcos_ref, dsin_ref):
    rows = lax.broadcasted_iota(jnp.int32, (CHANNELS, CHANNELS), 0)
    cols = lax.broadcasted_iota(jnp.int32, (CHANNELS, CHANNELS), 1)
    upto = (rows <= cols).astype(jnp.float32).astype(jnp.bfloat16)
    flags = jnp.broadcast_to(flags_ref[...].astype(jnp.float32), (16, CHANNELS)).astype(jnp.bfloat16)
    count = jnp.dot(flags, upto, preferred_element_type=jnp.float32)[0:1].astype(jnp.int32)
    ones = jnp.ones((CHANNELS, 128), jnp.bfloat16)

    def place(step, carry):
        row = lax.broadcasted_iota(jnp.int32, (64, CHANNELS), 0) + step * 64
        rank = (row & (OWNERS - 1)) * LIVE_DEV + (row >> 8)
        below = (count <= rank).astype(jnp.float32).astype(jnp.bfloat16)
        channel = jnp.dot(below, ones, preferred_element_type=jnp.float32).astype(jnp.int32)
        at = pl.ds(pl.multiple_of(step * 64, 64), 64)
        lane = lax.broadcasted_iota(jnp.int32, (64, 128), 1)
        c, s = unit_circle((channel * lane) & (FRAME - 1))
        scale = np.float32(1.0 / math.sqrt(FRAME))
        cos_ref[at, :] = c * scale
        sin_ref[at, :] = s * scale
        c, s = unit_circle((channel * 128) & (FRAME - 1))
        dcos_ref[at, :] = c
        dsin_ref[at, :] = s
        return carry

    lax.fori_loop(0, LIVE // 64, place, 0)

    def turn(step, carry):
        at = pl.ds(pl.multiple_of(step * 64, 64), 64)
        c, s = cos_ref[at, :], sin_ref[at, :]
        dc, ds = dcos_ref[at, :], dsin_ref[at, :]
        out = (step >> 2) * (2 * OWNERS) + (step & 3) * 64
        re = pl.ds(pl.multiple_of(out, 64), 64)
        im = pl.ds(pl.multiple_of(out + OWNERS, 64), 64)
        for v in range(FRAME // 128):
            table_ref[re, v * 128 : (v + 1) * 128] = c.astype(jnp.bfloat16)
            table_ref[im, v * 128 : (v + 1) * 128] = (-s).astype(jnp.bfloat16)
            if v < FRAME // 128 - 1:
                c, s = dc * c - ds * s, ds * c + dc * s
        return carry

    lax.fori_loop(0, LIVE // 64, turn, 0)


def late_kernel(volt_ref, window_ref, late_ref):
    def lanes(b, carry):
        lane = pl.multiple_of(b * 128, 128)

        def load(f, rows):
            return volt_ref[rows : rows + 16, pl.ds(pl.multiple_of(f * FRAME + lane, 128), 128)]

        def store(f, rows, value):
            at = (f - EARLY) * IN_DEV + rows
            late_ref[at : at + 16, pl.ds(lane, 128)] = value

        filter_block(window_ref, load, store, range(EARLY, FR_DEV), lane)
        return carry

    lax.fori_loop(0, FRAME // 128, lanes, 0)


def transposed_dot(a, b):
    return lax.dot_general(a, b, (((1,), (1,)), ((), ())), preferred_element_type=jnp.float32)


def spectra_kernel(halo_ref, volt_ref, window_ref, table_ref, late_ref, out_ref, early_ref, wide_ref):
    @pl.when(pl.program_id(0) == 0)
    def _():
        def lanes(b, carry):
            lane = pl.multiple_of(b * 128, 128)

            def load(f, rows):
                ref, g = (halo_ref, f + TAPS - 1) if f < 0 else (volt_ref, f)
                return ref[rows : rows + 16, pl.ds(pl.multiple_of(g * FRAME + lane, 128), 128)]

            def store(f, rows, value):
                at = f * IN_DEV + rows
                early_ref[at : at + 16, pl.ds(lane, 128)] = value

            filter_block(window_ref, load, store, range(EARLY), lane)
            return carry

        lax.fori_loop(0, FRAME // 128, lanes, 0)

    for n in range(PAIRS // 2):
        block = early_ref[...] if n == 0 else late_ref[(n - 1) * 256 : n * 256, :]
        both = transposed_dot(table_ref[...], block)
        for r in range(2):
            for h in range(2):
                value = both[r * OWNERS : (r + 1) * OWNERS, h * 128 : (h + 1) * 128]
                wide_ref[pl.ds(r * PAIRS + 2 * n + h, OWNERS, 2 * PAIRS), :] = value
    out_ref[...] = wide_ref[...].reshape(OWNERS, 2 * PAIRS, 128).astype(jnp.bfloat16)


def beam_kernel(recv_ref, place_ref, position_ref, sub_ref, out_ref, x_ref, part_ref, beam_ref):
    low = lax.broadcasted_iota(jnp.int32, (2 * PAIRS, 128), 1) < IN_DEV

    def pairs(s, carry):
        lane = pl.multiple_of(s * 128, 128)
        for b in range(N_TM):
            one = recv_ref[2 * s * N_TM + b].astype(jnp.float32)
            two = recv_ref[(2 * s + 1) * N_TM + b].astype(jnp.float32)
            even = jnp.where(low, one, pltpu.roll(two, 64, 1))
            odd = jnp.where(low, pltpu.roll(one, 64, 1), two)
            x_ref[b * 32 : b * 32 + 16, pl.ds(lane, 128)] = even.astype(jnp.bfloat16)
            x_ref[b * 32 + 16 : b * 32 + 32, pl.ds(lane, 128)] = odd.astype(jnp.bfloat16)
        return carry

    lax.fori_loop(0, N_FEED // 2, pairs, 0)
    total = [None] * CYL
    for p in range(2):
        for y in range(CYL):
            at = slice((p * CYL + y) * NS, (p * CYL + y + 1) * NS)
            cells = jnp.dot(x_ref[...], place_ref[:, at], preferred_element_type=jnp.float32).astype(jnp.bfloat16)
            both = jnp.dot(cells, position_ref[...], preferred_element_type=jnp.float32)
            both = both.reshape(16, 2, PAIRS, 2 * NS)
            part_ref[y, :, 0] = both[:, 0, :, :NS] + both[:, 1, :, NS:]
            part_ref[y, :, 1] = both[:, 1, :, :NS] - both[:, 0, :, NS:]

        def join(f, carry):
            re = [part_ref[y, f, 0] for y in range(CYL)]
            im = [part_ref[y, f, 1] for y in range(CYL)]
            re_s, re_d = re[0] + re[2], re[0] - re[2]
            im_s, im_d = im[0] + im[2], im[0] - im[2]
            re_t, re_e = re[1] + re[3], re[1] - re[3]
            im_t, im_e = im[1] + im[3], im[1] - im[3]
            out_re = [re_s + re_t, re_d + im_e, re_s - re_t, re_d - im_e]
            out_im = [im_s + im_t, im_d - re_e, im_s - im_t, im_d + re_e]
            at = pl.ds(pl.multiple_of(f * 16, 16), 16)
            for e in range(CYL):
                value = jnp.concatenate([out_re[e], out_im[e]], axis=0) * 0.5
                beam_ref[at, e * NS : (e + 1) * NS] = value.astype(jnp.bfloat16)
            return carry

        lax.fori_loop(0, 16, join, 0)
        for e in range(CYL):
            up = jnp.dot(sub_ref[...], beam_ref[:, e * NS : (e + 1) * NS], preferred_element_type=jnp.float32)
            power = jnp.sum((up * up).reshape(2 * N_TM, UPCH, NS), axis=0)
            total[e] = power if p == 0 else total[e] + power
    for e in range(CYL):
        out_ref[0, :, e * NS : (e + 1) * NS] = total[e] * (1.0 / (2.0 * N_TM * (FR_DEV // UPCH)))


def cost(flops, nbytes):
    return pl.CostEstimate(flops=int(flops), bytes_accessed=int(nbytes), transcendentals=0)


def whole(shape, *index):
    index = index or (0,) * len(shape)
    return pl.BlockSpec(shape, lambda *_: index)


def local(voltages, feed_slot, channel_flags):
    bf16, f32 = jnp.bfloat16, jnp.float32
    history = voltages[:, (FR_DEV - TAPS + 1) * FRAME :]
    halo = lax.ppermute(history, "tm", [(i, i + 1) for i in range(N_TM - 1)])
    window = jnp.asarray(window_table())
    late_rows = (FR_DEV - EARLY) * IN_DEV
    early_rows = EARLY * IN_DEV
    params = pltpu.CompilerParams(vmem_limit_bytes=32 * MIB)
    table = pl.pallas_call(
        table_kernel,
        name="channel_table",
        out_shape=jax.ShapeDtypeStruct((2 * LIVE, FRAME), bf16),
        scratch_shapes=[pltpu.VMEM((LIVE, 128), f32)] * 4,
        compiler_params=params,
        cost_estimate=cost(4e9, 6 * MIB),
    )(channel_flags.reshape(1, CHANNELS))
    late = pl.pallas_call(
        late_kernel,
        name="filter",
        out_shape=jax.ShapeDtypeStruct((late_rows, FRAME), bf16),
        compiler_params=params,
        cost_estimate=cost(4e9, 7 * MIB),
    )(voltages, window)
    sent = pl.pallas_call(
        spectra_kernel,
        name="spectra",
        grid=(LIVE_DEV,),
        in_specs=[
            whole((IN_DEV, (TAPS - 1) * FRAME)),
            whole((IN_DEV, EARLY * FRAME)),
            whole((TAPS, FRAME)),
            pl.BlockSpec((2 * OWNERS, FRAME), lambda c: (c, 0)),
            whole((late_rows, FRAME)),
        ],
        out_specs=pl.BlockSpec((OWNERS, 2 * PAIRS, 128), lambda c: (0, c, 0)),
        out_shape=pltpu.HBM((OWNERS, LIVE_DEV * 2 * PAIRS, 128), bf16),
        scratch_shapes=[
            pltpu.VMEM((early_rows, FRAME), bf16),
            pltpu.VMEM((OWNERS * 2 * PAIRS, 128), f32),
        ],
        compiler_params=params,
        cost_estimate=cost(7e9, 14 * MIB),
    )(halo, voltages, window, table, late)
    got = lax.all_to_all(sent, ("feed", "tm"), split_axis=0, concat_axis=0, tiled=True)
    inputs = N_FEED * IN_DEV
    place = (feed_slot[:, None] == jnp.arange(inputs, dtype=jnp.int32)[None, :]).astype(bf16)
    return pl.pallas_call(
        beam_kernel,
        name="beams_and_power",
        grid=(LIVE_DEV,),
        in_specs=[
            pl.BlockSpec((OWNERS, 2 * PAIRS, 128), lambda c: (0, c, 0)),
            whole((inputs, inputs)),
            whole((NS, 2 * NS)),
            whole((256, 256)),
        ],
        out_specs=pl.BlockSpec((1, UPCH, CYL * NS), lambda c: (c, 0, 0)),
        out_shape=jax.ShapeDtypeStruct((LIVE_DEV, UPCH, CYL * NS), f32),
        scratch_shapes=[
            pltpu.VMEM((256, inputs), bf16),
            pltpu.VMEM((CYL, 16, 2, PAIRS, NS), f32),
            pltpu.VMEM((256, CYL * NS), bf16),
        ],
        compiler_params=pltpu.CompilerParams(vmem_limit_bytes=36 * MIB),
        cost_estimate=cost(9e9, 14 * MIB),
    )(got, place, jnp.asarray(position_table(), dtype=bf16), jnp.asarray(sub_channel_table(), dtype=bf16))


def solution(mesh):
    in_specs = (P("feed", "tm"), P(), P())
    out_specs = P(("feed", "tm"), None, None)
    return jax.shard_map(local, mesh=mesh, in_specs=in_specs, out_specs=out_specs, check_vma=False)
```

time: 173 us -> 146 us (0.84)
  starting transfers between devices: 42 us -> 18.6 us
  waiting for transfers between devices: 53.6 us -> 70.5 us
  local copies, waits for them, and re-layouts: 22.9 us -> 7.53 us
  Pallas kernels: 51.2 us -> 44.5 us
  other arithmetic: 2.24 us -> 4.64 us
    all_to_all x6 -> x1, starting transfers between devices: 37.4 us -> 14 us  [local(): lax.all_to_all(sent, ('feed', 'tm'), split_axis=0, concat_axis=0, tiled=T...]
    all_to_all x6 -> x1, waiting for transfers between devices: 53.6 us -> 70.5 us  [local(): lax.all_to_all(sent, ('feed', 'tm'), split_axis=0, concat_axis=0, tiled=T...]
    unnamed x36 -> x18, local copies, waits for them, and re-layouts: 21.7 us -> 6.35 us
    pallas_call x7 -> x4, Pallas kernels: 51.2 us -> 44.5 us  [the longest x1 26.3 us: local(): pl.pallas_call(beam_kernel, name='beams_and_power', grid=(LIVE_DEV,), in_...]
    convert_element_type x1, other arithmetic: 1.41 us -> 4.64 us  [local(): (feed_slot[:, None] == jnp.arange(inputs, dtype=jnp.int32)[None, :]).asty...]
  transfers between devices with their start and end apart: 7 -> 2, of which waited for: 4 -> 1; matrix products, arithmetic and copies ran while one was open for 1% -> 3% of each run, Pallas kernels for 28% -> 5%
where the time goes in v1:
time: 146 us
  waiting for transfers between devices  70.5 us (48%)
  Pallas kernels  44.5 us (30%)
  starting transfers between devices  18.6 us (13%)
  local copies, waits for them, and re-layouts  7.53 us (5%)
  other arithmetic  4.64 us (3%)
    all_to_all x1, waiting for transfers between devices, local(): lax.all_to_all(sent, ('feed', 'tm'), split_axis=0, concat_axis=0, tiled=T...  70.5 us
    pallas_call x1, Pallas kernels, local(): pl.pallas_call(beam_kernel, name='beams_and_power', grid=(LIVE_DEV,), in_...  26.3 us
    all_to_all x1, starting transfers between devices, local(): lax.all_to_all(sent, ('feed', 'tm'), split_axis=0, concat_axis=0, tiled=T...  14 us
    pallas_call x1, Pallas kernels, local(): pl.pallas_call(spectra_kernel, name='spectra', grid=(LIVE_DEV,), in_specs...  10.3 us
    unnamed x18, local copies, waits for them, and re-layouts  6.35 us
    pallas_call x1, Pallas kernels, local(): pl.pallas_call(table_kernel, name='channel_table', out_shape=jax.ShapeDty...  5.95 us
    convert_element_type x1, other arithmetic, local(): (feed_slot[:, None] == jnp.arange(inputs, dtype=jnp.int32)[None, :]).asty...  4.64 us
    ppermute x1, starting transfers between devices, local(): halo = lax.ppermute(history, 'tm', [(i, i + 1) for i in range(N_TM - 1)])  4.59 us
  transfers between devices with their start and end apart: 2, of which 1 were waited for; matrix products, arithmetic and copies ran while one was open for 3% of the time, Pallas kernels for 5%

profile of v1, /device:TPU:1, one launch (start us, length us, event | category | flops | bytes accessed | tf_op | source)
XLA Modules:
  0.0 145.9 jit_solution(4586406352157916370)
XLA Ops:
  0.0 1.2 slice.3
  1.2 4.6 %collective-permute-start = (bf16[64,6144]{1,0:T(8,128)(2,1)S(1)}, bf16[64,6144]{1,0:T(8,128)(2,1)S(1)}, u32[]{:S(2)}, u32[]{:S(2)}) collective-permute-start(bf16[64,6144]{1,0:T(8,128)(2,1)S(1)} %slice.3), channel_id=1, source_target_pairs={{0,1},{1,2},{2,3},{3,4},{4,5},{5,6},{6,7},{8,9},{9,10},{10,11},{11... | collective-permute-start | bytes 2359304 | tf_op jit(solution)/shard_map/ppermute | solution.py:240
  5.8 0.0 copy-start.1
  5.8 2.2 %copy-done.1 = bf16[64,32768]{1,0:T(8,128)(2,1)S(1)} copy-done((bf16[64,32768]{1,0:T(8,128)(2,1)S(1)}, bf16[64,32768]{1,0:T(8,128)(2,1)}, u32[]{:S(2)}) %copy-start.1) | copy-done | bytes 4194328
  8.0 0.0 copy-start.6
  8.0 0.8 copy-done.6
  8.7 0.0 copy-start.3
  8.7 2.0 %filter.1.late_ref = bf16[768,2048]{1,0:T(8,128)(2,1)S(1)} custom-call(bf16[64,32768]{1,0:T(8,128)(2,1)S(1)} %copy-done.1, f32[4,2048]{1,0:T(4,128)S(1)} %copy-done.6), custom_call_target="tpu_custom_call" | custom-call | flops 4000000000 | bytes 7340032 | tf_op jit(solution)/shard_map/filter/pallas_call | solution.py:253
  10.8 0.0 copy-done.3
  10.8 0.0 copy-start.2
  10.8 0.0 copy-start.7
  10.8 5.9 %channel_table.1.table_ref = bf16[1536,2048]{1,0:T(8,128)(2,1)S(1)} custom-call(s32[1,1024]{1,0:T(1,128)S(1)} %bitcast.1), custom_call_target="tpu_custom_call" | custom-call | flops 4000000000 | bytes 6291456 | tf_op jit(solution)/shard_map/channel_table/pallas_call | solution.py:245
  16.8 0.0 collective-permute-done.halo_ref
  16.8 0.0 copy-done.2
  16.8 0.0 copy-done.7
  16.8 10.3 %spectra.1 = bf16[256,48,128]{2,1,0:T(8,128)(2,1)} custom-call(bf16[64,6144]{1,0:T(8,128)(2,1)S(1)} %collective-permute-done.halo_ref, bf16[64,32768]{1,0:T(8,128)(2,1)S(1)} %copy-done.2, f32[4,2048]{1,0:T(4,128)S(1)} %copy-done.7, bf16[1536,2048]{1,0:T(8,128)(2,1)S(1)} %channel_table.1.table_ref, bf16[768,2048]{1,0:T(8,128)(2,1)S(1)} %filter.1.late_ref), custom_call_target="tpu_custom_call" | custom-call | flops 7000000000 | bytes 14680064 | tf_op jit(solution)/shard_map/spectra/pallas_call | solution.py:260
  27.1 14.0 %all-to-all-start = ((bf16[256,48,128]{2,1,0:T(8,128)(2,1)}), bf16[256,48,128]{2,1,0:T(8,128)(2,1)S(1)}, u32[]{:S(2)}, u32[]{:S(2)}) async-start(bf16[256,48,128]{2,1,0:T(8,128)(2,1)} %spectra.1), calls=%async_computation | async-start | bytes 6291456 | tf_op jit(solution)/shard_map/all_to_all | solution.py:280
  41.0 0.0 copy-done.8
  41.1 4.6 %fusion.place_ref = bf16[2048,2048]{1,0:T(8,128)(2,1)} fusion(s32[2048]{0:T(1024)S(1)} %copy-done.8), kind=kLoop, calls=%fused_computation.1 | loop fusion | flops 8388608 | bytes 8396800 | tf_op jit(solution)/shard_map/convert_element_type | solution.py:282
  45.7 70.5 %all-to-all-done.recv_ref = bf16[256,48,128]{2,1,0:T(8,128)(2,1)S(1)} async-done(((bf16[256,48,128]{2,1,0:T(8,128)(2,1)}), bf16[256,48,128]{2,1,0:T(8,128)(2,1)S(1)}, u32[]{:S(2)}, u32[]{:S(2)}) %all-to-all-start) | async-done | bytes 3145760 | tf_op jit(solution)/shard_map/all_to_all | solution.py:280
  116.2 0.0 copy-done.4
  116.2 0.0 copy-done.5
  116.2 3.4 %copy-done = bf16[2048,2048]{1,0:T(8,128)(2,1)S(1)} copy-done((bf16[2048,2048]{1,0:T(8,128)(2,1)S(1)}, bf16[2048,2048]{1,0:T(8,128)(2,1)}, u32[]{:S(2)}) %copy-start) | copy-done | bytes 8388632
  119.6 26.3 %beams_and_power.1 = f32[3,16,1024]{2,1,0:T(8,128)} custom-call(bf16[256,48,128]{2,1,0:T(8,128)(2,1)S(1)} %all-to-all-done.recv_ref, bf16[2048,2048]{1,0:T(8,128)(2,1)S(1)} %copy-done, bf16[256,512]{1,0:T(8,128)(2,1)S(1)} %copy-done.4, bf16[256,256]{1,0:T(8,128)(2,1)S(1)} %copy-done.5), custom_call_target="tpu_custom_call" | custom-call | flops 8999999488 | bytes 14680064 | tf_op jit(solution)/shard_map/beams_and_power/pallas_call | solution.py:283
  (4 shorter events, 0.0 us)
Async XLA Ops:
  1.2 15.6 %collective-permute-start = (bf16[64,6144]{1,0:T(8,128)(2,1)S(1)}, bf16[64,6144]{1,0:T(8,128)(2,1)S(1)}, u32[]{:S(2)}, u32[]{:S(2)}) collective-permute-start(bf16[64,6144]{1,0:T(8,128)(2,1)S(1)} %slice.3), channel_id=1, source_target_pairs={{0,1},{1,2},{2,3},{3,4},{4,5},{5,6},{6,7},{8,9},{9,10},{10,11},{11... | collective-permute-start | bytes 2359304 | tf_op jit(solution)/shard_map/ppermute | solution.py:240
  5.8 2.2 %copy-start.1 = (bf16[64,32768]{1,0:T(8,128)(2,1)S(1)}, bf16[64,32768]{1,0:T(8,128)(2,1)}, u32[]{:S(2)}) copy-start(bf16[64,32768]{1,0:T(8,128)(2,1)} %volt_ref.3) | copy-start | bytes 12582916
  8.0 0.8 copy-start.6
  8.7 2.0 %copy-start.3 = (s32[1024]{0:T(1024)S(1)}, s32[1024]{0:T(1024)}, u32[]{:S(2)}) copy-start(s32[1024]{0:T(1024)} %param.8) | copy-start | bytes 12292
  10.8 6.0 %copy-start.2 = (bf16[64,32768]{1,0:T(8,128)(2,1)S(1)}, bf16[64,32768]{1,0:T(8,128)(2,1)}, u32[]{:S(2)}) copy-start(bf16[64,32768]{1,0:T(8,128)(2,1)} %volt_ref.3) | copy-start | bytes 12582916
  10.8 6.0 %copy-start.7 = (f32[4,2048]{1,0:T(4,128)S(1)}, f32[4,2048]{1,0:T(4,128)}, u32[]{:S(2)}) copy-start(f32[4,2048]{1,0:T(4,128)} %constant.6.clone.window_ref) | copy-start | bytes 98308
  27.1 14.0 %copy-start.8 = (s32[2048]{0:T(1024)S(1)}, s32[2048]{0:T(1024)}, u32[]{:S(2)}) copy-start(s32[2048]{0:T(1024)} %param.7) | copy-start | bytes 24580
  27.1 89.2 %copy-start.4 = (bf16[256,512]{1,0:T(8,128)(2,1)S(1)}, bf16[256,512]{1,0:T(8,128)(2,1)}, u32[]{:S(2)}) copy-start(bf16[256,512]{1,0:T(8,128)(2,1)} %constant.7.clone.position_ref) | copy-start | bytes 786436
  27.1 89.2 %copy-start.5 = (bf16[256,256]{1,0:T(8,128)(2,1)S(1)}, bf16[256,256]{1,0:T(8,128)(2,1)}, u32[]{:S(2)}) copy-start(bf16[256,256]{1,0:T(8,128)(2,1)} %constant.8.clone.sub_ref) | copy-start | bytes 393220
  27.1 89.2 %all-to-all-start = ((bf16[256,48,128]{2,1,0:T(8,128)(2,1)}), bf16[256,48,128]{2,1,0:T(8,128)(2,1)S(1)}, u32[]{:S(2)}, u32[]{:S(2)}) async-start(bf16[256,48,128]{2,1,0:T(8,128)(2,1)} %spectra.1), calls=%async_computation | async-start | bytes 6291456 | tf_op jit(solution)/shard_map/all_to_all | solution.py:280
  116.2 3.4 %copy-start = (bf16[2048,2048]{1,0:T(8,128)(2,1)S(1)}, bf16[2048,2048]{1,0:T(8,128)(2,1)}, u32[]{:S(2)}) copy-start(bf16[2048,2048]{1,0:T(8,128)(2,1)} %fusion.place_ref) | copy-start | bytes 25165828

commit v2 on v1

--- a/solution.py
+++ b/solution.py
@@ -43,7 +43,7 @@
 
 def position_table():
     cosine, sine = cos_sin(NS, NS, NS)
-    return np.concatenate([cosine, sine], axis=1)
+    return np.block([[cosine, -sine], [sine, cosine]])
 
 
 def sub_channel_table():
@@ -83,21 +83,29 @@
             store(f, rows, total.astype(jnp.bfloat16))
 
 
-def table_kernel(flags_ref, table_ref, cos_ref, sin_ref, dcos_ref, dsin_ref):
-    rows = lax.broadcasted_iota(jnp.int32, (CHANNELS, CHANNELS), 0)
-    cols = lax.broadcasted_iota(jnp.int32, (CHANNELS, CHANNELS), 1)
-    upto = (rows <= cols).astype(jnp.float32).astype(jnp.bfloat16)
-    flags = jnp.broadcast_to(flags_ref[...].astype(jnp.float32), (16, CHANNELS)).astype(jnp.bfloat16)
-    count = jnp.dot(flags, upto, preferred_element_type=jnp.float32)[0:1].astype(jnp.int32)
-    ones = jnp.ones((CHANNELS, 128), jnp.bfloat16)
+def table_kernel(flags_ref, table_ref, cos_ref, sin_ref, dcos_ref, dsin_ref, sign_ref):
+    lane = lax.broadcasted_iota(jnp.int32, (64, 128), 1)
+    upto = (lax.broadcasted_iota(jnp.int32, (128, 128), 0) <= lax.broadcasted_iota(jnp.int32, (128, 128), 1)).astype(
+        jnp.float32
+    )
+    ones = jnp.ones((128, 128), jnp.float32)
+    sums = jnp.concatenate([upto, ones], axis=1).astype(jnp.bfloat16)
+    ones = ones.astype(jnp.bfloat16)
+    flags = flags_ref[...].astype(jnp.float32)
+    flags = jnp.concatenate([flags, jnp.zeros_like(flags)], axis=0).astype(jnp.bfloat16)
+    count = jnp.dot(flags, sums, preferred_element_type=jnp.float32)
+    earlier = jnp.zeros((1, 128), jnp.float32)
+    counts = []
+    for r in range(CHANNELS // 128):
+        counts.append((count[r : r + 1, :128] + earlier).astype(jnp.int32))
+        earlier = earlier + count[r : r + 1, 128:]
 
     def place(step, carry):
-        row = lax.broadcasted_iota(jnp.int32, (64, CHANNELS), 0) + step * 64
+        row = lax.broadcasted_iota(jnp.int32, (64, 128), 0) + step * 64
         rank = (row & (OWNERS - 1)) * LIVE_DEV + (row >> 8)
-        below = (count <= rank).astype(jnp.float32).astype(jnp.bfloat16)
+        below = sum((c <= rank).astype(jnp.float32) for c in counts).astype(jnp.bfloat16)
         channel = jnp.dot(below, ones, preferred_element_type=jnp.float32).astype(jnp.int32)
         at = pl.ds(pl.multiple_of(step * 64, 64), 64)
-        lane = lax.broadcasted_iota(jnp.int32, (64, 128), 1)
         c, s = unit_circle((channel * lane) & (FRAME - 1))
         scale = np.float32(1.0 / math.sqrt(FRAME))
         cos_ref[at, :] = c * scale
@@ -105,6 +113,7 @@
         c, s = unit_circle((channel * 128) & (FRAME - 1))
         dcos_ref[at, :] = c
         dsin_ref[at, :] = s
+        sign_ref[at, :] = (1 - 2 * (channel & 1)).astype(jnp.float32)
         return carry
 
     lax.fori_loop(0, LIVE // 64, place, 0)
@@ -113,20 +122,25 @@
         at = pl.ds(pl.multiple_of(step * 64, 64), 64)
         c, s = cos_ref[at, :], sin_ref[at, :]
         dc, ds = dcos_ref[at, :], dsin_ref[at, :]
+        sign = sign_ref[at, :].astype(jnp.bfloat16)
         out = (step >> 2) * (2 * OWNERS) + (step & 3) * 64
         re = pl.ds(pl.multiple_of(out, 64), 64)
         im = pl.ds(pl.multiple_of(out + OWNERS, 64), 64)
-        for v in range(FRAME // 128):
-            table_ref[re, v * 128 : (v + 1) * 128] = c.astype(jnp.bfloat16)
-            table_ref[im, v * 128 : (v + 1) * 128] = (-s).astype(jnp.bfloat16)
-            if v < FRAME // 128 - 1:
+        half = FRAME // 256
+        for v in range(half):
+            cb, sb = c.astype(jnp.bfloat16), (-s).astype(jnp.bfloat16)
+            table_ref[re, v * 128 : (v + 1) * 128] = cb
+            table_ref[im, v * 128 : (v + 1) * 128] = sb
+            table_ref[re, (v + half) * 128 : (v + half + 1) * 128] = cb * sign
+            table_ref[im, (v + half) * 128 : (v + half + 1) * 128] = sb * sign
+            if v < half - 1:
                 c, s = dc * c - ds * s, ds * c + dc * s
         return carry
 
     lax.fori_loop(0, LIVE // 64, turn, 0)
 
 
-def late_kernel(volt_ref, window_ref, late_ref):
+def late_kernel(volt_ref, window_ref, _, late_ref):
     def lanes(b, carry):
         lane = pl.multiple_of(b * 128, 128)
 
@@ -166,9 +180,10 @@
 
         lax.fori_loop(0, FRAME // 128, lanes, 0)
 
+    table = table_ref[pl.ds(pl.multiple_of(pl.program_id(0) * 2 * OWNERS, 2 * OWNERS), 2 * OWNERS), :]
     for n in range(PAIRS // 2):
         block = early_ref[...] if n == 0 else late_ref[(n - 1) * 256 : n * 256, :]
-        both = transposed_dot(table_ref[...], block)
+        both = transposed_dot(table, block)
         for r in range(2):
             for h in range(2):
                 value = both[r * OWNERS : (r + 1) * OWNERS, h * 128 : (h + 1) * 128]
@@ -176,53 +191,63 @@
     out_ref[...] = wide_ref[...].reshape(OWNERS, 2 * PAIRS, 128).astype(jnp.bfloat16)
 
 
-def beam_kernel(recv_ref, place_ref, position_ref, sub_ref, out_ref, x_ref, part_ref, beam_ref):
+def beam_kernel(recv_ref, slot_ref, position_ref, sub_ref, out_ref, x_ref, place_ref, cell_ref, part_ref, beam_ref):
     low = lax.broadcasted_iota(jnp.int32, (2 * PAIRS, 128), 1) < IN_DEV
+    groups = 2 * CYL
 
     def pairs(s, carry):
         lane = pl.multiple_of(s * 128, 128)
-        for b in range(N_TM):
-            one = recv_ref[2 * s * N_TM + b].astype(jnp.float32)
-            two = recv_ref[(2 * s + 1) * N_TM + b].astype(jnp.float32)
-            even = jnp.where(low, one, pltpu.roll(two, 64, 1))
-            odd = jnp.where(low, pltpu.roll(one, 64, 1), two)
-            x_ref[b * 32 : b * 32 + 16, pl.ds(lane, 128)] = even.astype(jnp.bfloat16)
-            x_ref[b * 32 + 16 : b * 32 + 32, pl.ds(lane, 128)] = odd.astype(jnp.bfloat16)
+        for c in range(LIVE_DEV):
+            for b in range(N_TM):
+                part = slice(c * 2 * PAIRS, (c + 1) * 2 * PAIRS)
+                one = recv_ref[2 * s * N_TM + b, part].astype(jnp.float32)
+                two = recv_ref[(2 * s + 1) * N_TM + b, part].astype(jnp.float32)
+                even = jnp.where(low, one, pltpu.roll(two, 64, 1))
+                odd = jnp.where(low, pltpu.roll(one, 64, 1), two)
+                row = c * 256 + b * 32
+                x_ref[row : row + 16, pl.ds(lane, 128)] = even.astype(jnp.bfloat16)
+                x_ref[row + 16 : row + 32, pl.ds(lane, 128)] = odd.astype(jnp.bfloat16)
         return carry
 
     lax.fori_loop(0, N_FEED // 2, pairs, 0)
-    total = [None] * CYL
+    slot = jnp.concatenate([slot_ref[...]] * 2, axis=1)
+    for i in range(groups):
+        want = lax.broadcasted_iota(jnp.int32, slot.shape, 1) + i * NS
+        place_ref[i % 2] = (slot == want).astype(jnp.float32).astype(jnp.bfloat16)
+        cells = jnp.dot(x_ref[...], place_ref[i % 2], preferred_element_type=jnp.float32)
+        cells = cells.reshape(-1, 2, PAIRS, NS)
+        both = [cells[:, r].reshape(-1, NS) for r in range(2)]
+        cell_ref[i] = jnp.concatenate(both, axis=1).astype(jnp.bfloat16)
+    for i in range(groups):
+        part_ref[i] = jnp.dot(cell_ref[i], position_ref[...], preferred_element_type=jnp.float32)
     for p in range(2):
-        for y in range(CYL):
-            at = slice((p * CYL + y) * NS, (p * CYL + y + 1) * NS)
-            cells = jnp.dot(x_ref[...], place_ref[:, at], preferred_element_type=jnp.float32).astype(jnp.bfloat16)
-            both = jnp.dot(cells, position_ref[...], preferred_element_type=jnp.float32)
-            both = both.reshape(16, 2, PAIRS, 2 * NS)
-            part_ref[y, :, 0] = both[:, 0, :, :NS] + both[:, 1, :, NS:]
-            part_ref[y, :, 1] = both[:, 1, :, :NS] - both[:, 0, :, NS:]
 
         def join(f, carry):
-            re = [part_ref[y, f, 0] for y in range(CYL)]
-            im = [part_ref[y, f, 1] for y in range(CYL)]
+            rows = pl.ds(pl.multiple_of(f * PAIRS, PAIRS), PAIRS)
+            re = [part_ref[p * CYL + y, rows, :NS] for y in range(CYL)]
+            im = [part_ref[p * CYL + y, rows, NS:] for y in range(CYL)]
             re_s, re_d = re[0] + re[2], re[0] - re[2]
             im_s, im_d = im[0] + im[2], im[0] - im[2]
             re_t, re_e = re[1] + re[3], re[1] - re[3]
             im_t, im_e = im[1] + im[3], im[1] - im[3]
             out_re = [re_s + re_t, re_d + im_e, re_s - re_t, re_d - im_e]
             out_im = [im_s + im_t, im_d - re_e, im_s - im_t, im_d + re_e]
-            at = pl.ds(pl.multiple_of(f * 16, 16), 16)
+            at = pl.ds(pl.multiple_of(f * 2 * PAIRS, 2 * PAIRS), 2 * PAIRS)
             for e in range(CYL):
                 value = jnp.concatenate([out_re[e], out_im[e]], axis=0) * 0.5
-                beam_ref[at, e * NS : (e + 1) * NS] = value.astype(jnp.bfloat16)
+                beam_ref[p, at, e * NS : (e + 1) * NS] = value.astype(jnp.bfloat16)
             return carry
 
-        lax.fori_loop(0, 16, join, 0)
+        lax.fori_loop(0, LIVE_DEV * 16, join, 0, unroll=2)
+    for c in range(LIVE_DEV):
         for e in range(CYL):
-            up = jnp.dot(sub_ref[...], beam_ref[:, e * NS : (e + 1) * NS], preferred_element_type=jnp.float32)
-            power = jnp.sum((up * up).reshape(2 * N_TM, UPCH, NS), axis=0)
-            total[e] = power if p == 0 else total[e] + power
-    for e in range(CYL):
-        out_ref[0, :, e * NS : (e + 1) * NS] = total[e] * (1.0 / (2.0 * N_TM * (FR_DEV // UPCH)))
+            total = None
+            for p in range(2):
+                beams = beam_ref[p, c * 256 : (c + 1) * 256, e * NS : (e + 1) * NS]
+                up = jnp.dot(sub_ref[...], beams, preferred_element_type=jnp.float32)
+                power = jnp.sum((up * up).reshape(2 * N_TM, UPCH, NS), axis=0)
+                total = power if p == 0 else total + power
+            out_ref[c, :, e * NS : (e + 1) * NS] = total * (1.0 / (2.0 * N_TM * (FR_DEV // UPCH)))
 
 
 def cost(flops, nbytes):
@@ -239,6 +264,7 @@
     history = voltages[:, (FR_DEV - TAPS + 1) * FRAME :]
     halo = lax.ppermute(history, "tm", [(i, i + 1) for i in range(N_TM - 1)])
     window = jnp.asarray(window_table())
+    in_vmem = pl.BlockSpec(memory_space=pltpu.VMEM)
     late_rows = (FR_DEV - EARLY) * IN_DEV
     early_rows = EARLY * IN_DEV
     params = pltpu.CompilerParams(vmem_limit_bytes=32 * MIB)
@@ -246,27 +272,28 @@
         table_kernel,
         name="channel_table",
         out_shape=jax.ShapeDtypeStruct((2 * LIVE, FRAME), bf16),
-        scratch_shapes=[pltpu.VMEM((LIVE, 128), f32)] * 4,
+        scratch_shapes=[pltpu.VMEM((LIVE, 128), f32)] * 5,
         compiler_params=params,
         cost_estimate=cost(4e9, 6 * MIB),
-    )(channel_flags.reshape(1, CHANNELS))
+    )(channel_flags.reshape(CHANNELS // 128, 128))
     late = pl.pallas_call(
         late_kernel,
         name="filter",
+        in_specs=[in_vmem, in_vmem, pl.BlockSpec(memory_space=pl.ANY)],
         out_shape=jax.ShapeDtypeStruct((late_rows, FRAME), bf16),
         compiler_params=params,
         cost_estimate=cost(4e9, 7 * MIB),
-    )(voltages, window)
+    )(voltages, window, table)
     sent = pl.pallas_call(
         spectra_kernel,
         name="spectra",
         grid=(LIVE_DEV,),
         in_specs=[
-            whole((IN_DEV, (TAPS - 1) * FRAME)),
+            in_vmem,
             whole((IN_DEV, EARLY * FRAME)),
-            whole((TAPS, FRAME)),
-            pl.BlockSpec((2 * OWNERS, FRAME), lambda c: (c, 0)),
-            whole((late_rows, FRAME)),
+            in_vmem,
+            in_vmem,
+            in_vmem,
         ],
         out_specs=pl.BlockSpec((OWNERS, 2 * PAIRS, 128), lambda c: (0, c, 0)),
         out_shape=pltpu.HBM((OWNERS, LIVE_DEV * 2 * PAIRS, 128), bf16),
@@ -279,27 +306,28 @@
     )(halo, voltages, window, table, late)
     got = lax.all_to_all(sent, ("feed", "tm"), split_axis=0, concat_axis=0, tiled=True)
     inputs = N_FEED * IN_DEV
-    place = (feed_slot[:, None] == jnp.arange(inputs, dtype=jnp.int32)[None, :]).astype(bf16)
+    rows = LIVE_DEV * 256
     return pl.pallas_call(
         beam_kernel,
         name="beams_and_power",
-        grid=(LIVE_DEV,),
-        in_specs=[
-            pl.BlockSpec((OWNERS, 2 * PAIRS, 128), lambda c: (0, c, 0)),
-            whole((inputs, inputs)),
-            whole((NS, 2 * NS)),
-            whole((256, 256)),
-        ],
-        out_specs=pl.BlockSpec((1, UPCH, CYL * NS), lambda c: (c, 0, 0)),
+        in_specs=[in_vmem] * 4,
+        out_specs=in_vmem,
         out_shape=jax.ShapeDtypeStruct((LIVE_DEV, UPCH, CYL * NS), f32),
         scratch_shapes=[
-            pltpu.VMEM((256, inputs), bf16),
-            pltpu.VMEM((CYL, 16, 2, PAIRS, NS), f32),
-            pltpu.VMEM((256, CYL * NS), bf16),
+            pltpu.VMEM((rows, inputs), bf16),
+            pltpu.VMEM((2, inputs, NS), bf16),
+            pltpu.VMEM((2 * CYL, rows // 2, 2 * NS), bf16),
+            pltpu.VMEM((2 * CYL, rows // 2, 2 * NS), f32),
+            pltpu.VMEM((2, rows, CYL * NS), bf16),
         ],
         compiler_params=pltpu.CompilerParams(vmem_limit_bytes=36 * MIB),
-        cost_estimate=cost(9e9, 14 * MIB),
-    )(got, place, jnp.asarray(position_table(), dtype=bf16), jnp.asarray(sub_channel_table(), dtype=bf16))
+        cost_estimate=cost(9e9, 6 * MIB),
+    )(
+        got,
+        jnp.broadcast_to(feed_slot[:, None], (inputs, 128)),
+        jnp.asarray(position_table(), dtype=bf16),
+        jnp.asarray(sub_channel_table(), dtype=bf16),
+    )
 
 
 def solution(mesh):

time: 146 us -> 129 us (0.88)
  blocking collectives: 0 us -> 90.7 us
  waiting for transfers between devices: 70.5 us -> 0.75 us
  starting transfers between devices: 18.6 us -> 4.59 us
  Pallas kernels: 44.5 us -> 30.9 us
  local copies, waits for them, and re-layouts: 7.53 us -> 2.21 us
  other arithmetic: 4.64 us -> 0 us
    all_to_all x0 -> x1, blocking collectives: none -> 90.7 us  [local(): lax.all_to_all(sent, ('feed', 'tm'), split_axis=0, concat_axis=0, tiled=T...]
    all_to_all x1 -> x0, waiting for transfers between devices: 70.5 us -> none  [local(): lax.all_to_all(sent, ('feed', 'tm'), split_axis=0, concat_axis=0, tiled=T...]
    all_to_all x1 -> x0, starting transfers between devices: 14 us -> none  [local(): lax.all_to_all(sent, ('feed', 'tm'), split_axis=0, concat_axis=0, tiled=T...]
    pallas_call x2, Pallas kernels: 28.3 us -> 15.2 us  [the longest x1 13.2 us: local(): pl.pallas_call(beam_kernel, name='beams_and_power', in_specs=[in_vmem] *...]
    unnamed x18 -> x12, local copies, waits for them, and re-layouts: 6.35 us -> 0.7 us
    convert_element_type x1 -> x0, other arithmetic: 4.64 us -> none  [local(): (feed_slot[:, None] == jnp.arange(inputs, dtype=jnp.int32)[None, :]).asty...]
  transfers between devices with their start and end apart: 2 -> 1, of which waited for: 1 -> 1; matrix products, arithmetic and copies ran while one was open for 3% -> 0% of each run, Pallas kernels for 5% -> 6%
where the time goes in v2:
time: 129 us
  blocking collectives  90.7 us (70%)
  Pallas kernels  30.9 us (24%)
  starting transfers between devices  4.59 us (4%)
  local copies, waits for them, and re-layouts  2.21 us (2%)
    all_to_all x1, blocking collectives, local(): lax.all_to_all(sent, ('feed', 'tm'), split_axis=0, concat_axis=0, tiled=T...  90.7 us
    pallas_call x1, Pallas kernels, local(): pl.pallas_call(beam_kernel, name='beams_and_power', in_specs=[in_vmem] *...  13.2 us
    pallas_call x1, Pallas kernels, local(): pl.pallas_call(spectra_kernel, name='spectra', grid=(LIVE_DEV,), in_specs...  10.3 us
    pallas_call x1, Pallas kernels, local(): pl.pallas_call(table_kernel, name='channel_table', out_shape=jax.ShapeDty...  5.4 us
    ppermute x1, starting transfers between devices, local(): halo = lax.ppermute(history, 'tm', [(i, i + 1) for i in range(N_TM - 1)])  4.59 us
  transfers between devices with their start and end apart: 1, of which 1 were waited for; matrix products, arithmetic and copies ran while one was open for 0% of the time, Pallas kernels for 6%

profile of v2, /device:TPU:1, one launch (start us, length us, event | category | flops | bytes accessed | tf_op | source)
XLA Modules:
  0.0 129.2 jit_solution(7909106677612533083)
XLA Ops:
  0.0 1.2 slice.3
  1.2 4.6 %collective-permute-start = (bf16[64,6144]{1,0:T(8,128)(2,1)S(1)}, bf16[64,6144]{1,0:T(8,128)(2,1)S(1)}, u32[]{:S(2)}, u32[]{:S(2)}) collective-permute-start(bf16[64,6144]{1,0:T(8,128)(2,1)S(1)} %slice.3), channel_id=1, source_target_pairs={{0,1},{1,2},{2,3},{3,4},{4,5},{5,6},{6,7},{8,9},{9,10},{10,11},{11... | collective-permute-start | bytes 2359304 | tf_op jit(solution)/shard_map/ppermute | solution.py:265
  5.8 0.0 copy-start.1
  5.8 0.7 copy-done.1
  6.5 0.0 copy-start
  6.5 0.0 copy-start.4
  6.5 5.4 %channel_table.1._.table_ref = bf16[1536,2048]{1,0:T(8,128)(2,1)S(1)} custom-call(s32[8,128]{1,0:T(8,128)S(1)} %bitcast.1), custom_call_target="tpu_custom_call" | custom-call | flops 4000000000 | bytes 6291456 | tf_op jit(solution)/shard_map/channel_table/pallas_call | solution.py:271
  11.9 0.0 copy-done
  11.9 0.0 copy-done.4
  11.9 2.0 %filter.1.late_ref = bf16[768,2048]{1,0:T(8,128)(2,1)S(1)} custom-call(bf16[64,32768]{1,0:T(8,128)(2,1)S(1)} %copy-done, f32[4,2048]{1,0:T(4,128)S(1)} %copy-done.4, bf16[1536,2048]{1,0:T(8,128)(2,1)S(1)} %channel_table.1._.table_ref), custom_call_target="tpu_custom_call" | custom-call | flops 4000000000 | bytes 7340032 | tf_op jit(solution)/shard_map/filter/pallas_call | solution.py:279
  14.0 0.7 collective-permute-done.halo_ref
  14.7 10.3 %spectra.1 = bf16[256,48,128]{2,1,0:T(8,128)(2,1)} custom-call(bf16[64,6144]{1,0:T(8,128)(2,1)S(1)} %collective-permute-done.halo_ref, bf16[64,32768]{1,0:T(8,128)(2,1)S(1)} %copy-done, f32[4,2048]{1,0:T(4,128)S(1)} %copy-done.4, bf16[1536,2048]{1,0:T(8,128)(2,1)S(1)} %channel_table.1._.table_ref, bf16[768,2048]{1,0:T(8,128)(2,1)S(1)} %filter.1.late_ref), custom_call_target="tpu_custom_call" | custom-call | flops 7000000000 | bytes 14680064 | tf_op jit(solution)/shard_map/spectra/pallas_call | solution.py:287
  25.0 0.0 copy-start.5
  25.0 0.0 copy-start.2
  25.0 0.0 copy-start.3
  25.0 90.7 %all_to_all.5.recv_ref = bf16[256,48,128]{2,1,0:T(8,128)(2,1)S(1)} all-to-all(bf16[256,48,128]{2,1,0:T(8,128)(2,1)} %spectra.1), channel_id=1, replica_groups=mesh['feed'=32,'tm'=8] {'feed','tm'}, dimensions={0} | all-to-all | bytes 6291456 | tf_op jit(solution)/shard_map/all_to_all | solution.py:307
  115.7 0.0 copy-done.5
  115.7 0.3 broadcast_in_dim.2.slot_ref
  116.0 0.0 copy-done.2
  116.1 0.0 copy-done.3
  116.1 13.2 %beams_and_power.1 = f32[3,16,1024]{2,1,0:T(8,128)} custom-call(bf16[256,48,128]{2,1,0:T(8,128)(2,1)S(1)} %all_to_all.5.recv_ref, s32[2048,128]{1,0:T(8,128)S(1)} %broadcast_in_dim.2.slot_ref, bf16[512,512]{1,0:T(8,128)(2,1)S(1)} %copy-done.2, bf16[256,256]{1,0:T(8,128)(2,1)S(1)} %copy-done.3), custom_call_target="tpu_custom_call" | custom-call | flops 8999999488 | bytes 6291456 | tf_op jit(solution)/shard_map/beams_and_power/pallas_call | solution.py:310
Async XLA Ops:
  1.2 13.5 %collective-permute-start = (bf16[64,6144]{1,0:T(8,128)(2,1)S(1)}, bf16[64,6144]{1,0:T(8,128)(2,1)S(1)}, u32[]{:S(2)}, u32[]{:S(2)}) collective-permute-start(bf16[64,6144]{1,0:T(8,128)(2,1)S(1)} %slice.3), channel_id=1, source_target_pairs={{0,1},{1,2},{2,3},{3,4},{4,5},{5,6},{6,7},{8,9},{9,10},{10,11},{11... | collective-permute-start | bytes 2359304 | tf_op jit(solution)/shard_map/ppermute | solution.py:265
  5.8 0.7 copy-start.1
  6.5 5.4 %copy-start = (bf16[64,32768]{1,0:T(8,128)(2,1)S(1)}, bf16[64,32768]{1,0:T(8,128)(2,1)}, u32[]{:S(2)}) copy-start(bf16[64,32768]{1,0:T(8,128)(2,1)} %volt_ref.3) | copy-start | bytes 12582916
  6.5 5.4 %copy-start.4 = (f32[4,2048]{1,0:T(4,128)S(1)}, f32[4,2048]{1,0:T(4,128)}, u32[]{:S(2)}) copy-start(f32[4,2048]{1,0:T(4,128)} %constant.6.clone.window_ref) | copy-start | bytes 98308
  25.0 90.7 %copy-start.5 = (s32[2048]{0:T(1024)S(1)}, s32[2048]{0:T(1024)}, u32[]{:S(2)}) copy-start(s32[2048]{0:T(1024)} %param.7) | copy-start | bytes 24580
  25.0 91.0 %copy-start.2 = (bf16[512,512]{1,0:T(8,128)(2,1)S(1)}, bf16[512,512]{1,0:T(8,128)(2,1)}, u32[]{:S(2)}) copy-start(bf16[512,512]{1,0:T(8,128)(2,1)} %constant.7.clone.position_ref) | copy-start | bytes 1572868
  25.0 91.0 %copy-start.3 = (bf16[256,256]{1,0:T(8,128)(2,1)S(1)}, bf16[256,256]{1,0:T(8,128)(2,1)}, u32[]{:S(2)}) copy-start(bf16[256,256]{1,0:T(8,128)(2,1)} %constant.8.clone.sub_ref) | copy-start | bytes 393220

commit v3 on v2

--- a/solution.py
+++ b/solution.py
@@ -68,22 +68,38 @@
     return cosine, sine
 
 
-def filter_block(window_ref, load, store, frames, lane):
-    taps = [window_ref[pl.ds(t, 1), pl.ds(lane, 128)] for t in range(TAPS)]
-    for rows in range(0, IN_DEV, 16):
-        held = {}
-        for f in frames:
-            total = None
-            for t in range(TAPS):
-                g = f - TAPS + 1 + t
-                if g not in held:
-                    held[g] = load(g, rows).astype(jnp.float32)
-                term = taps[t] * held[g]
-                total = term if total is None else total + term
-            store(f, rows, total.astype(jnp.bfloat16))
-
-
-def table_kernel(flags_ref, table_ref, cos_ref, sin_ref, dcos_ref, dsin_ref, sign_ref):
+def fold_frames(window_ref, load, frames, even_ref, odd_ref, middle_ref, last_ref):
+    lane = lax.broadcasted_iota(jnp.int32, (16, 128), 1)
+    back = (128 - lane) & 127
+    last_ref[...] = jnp.zeros_like(last_ref)
+
+    def piece(v, carry):
+        sides = [pl.multiple_of(v * 128, 128), pl.multiple_of((FRAME // 128 - 1 - v) * 128, 128)]
+        taps = [[window_ref[pl.ds(t, 1), pl.ds(side, 128)] for t in range(TAPS)] for side in sides]
+        for rows in range(0, IN_DEV, 16):
+            held = [{}, {}]
+            for n, f in enumerate(frames):
+                total = [None, None]
+                for j in range(2):
+                    for t in range(TAPS):
+                        g = f - TAPS + 1 + t
+                        if g not in held[j]:
+                            held[j][g] = load(g, rows, sides[j]).astype(jnp.float32)
+                        term = taps[j][t] * held[j][g]
+                        total[j] = term if t == 0 else total[j] + term
+                at = slice(n * IN_DEV + rows, n * IN_DEV + rows + 16)
+                turned = jnp.take_along_axis(total[1], back, axis=1, mode="promise_in_bounds")
+                mirror = jnp.where(lane == 0, last_ref[at, :], turned)
+                last_ref[at, :] = turned
+                even_ref[at, pl.ds(sides[0], 128)] = (total[0] + mirror).astype(jnp.bfloat16)
+                odd_ref[at, pl.ds(sides[0], 128)] = (total[0] - mirror).astype(jnp.bfloat16)
+                middle_ref[at, :] = total[1].astype(jnp.bfloat16)
+        return carry
+
+    lax.fori_loop(0, FRAME // 256, piece, 0)
+
+
+def table_kernel(flags_ref, table_ref, sign_ref, cos_ref, sin_ref, dcos_ref, dsin_ref):
     lane = lax.broadcasted_iota(jnp.int32, (64, 128), 1)
     upto = (lax.broadcasted_iota(jnp.int32, (128, 128), 0) <= lax.broadcasted_iota(jnp.int32, (128, 128), 1)).astype(
         jnp.float32
@@ -113,7 +129,8 @@
         c, s = unit_circle((channel * 128) & (FRAME - 1))
         dcos_ref[at, :] = c
         dsin_ref[at, :] = s
-        sign_ref[at, :] = (1 - 2 * (channel & 1)).astype(jnp.float32)
+        sign = (1 - 2 * (channel & 1)).astype(jnp.float32) * scale
+        sign_ref[at, :] = jnp.where(lane == 0, sign, 0.0).astype(jnp.bfloat16)
         return carry
 
     lax.fori_loop(0, LIVE // 64, place, 0)
@@ -122,73 +139,70 @@
         at = pl.ds(pl.multiple_of(step * 64, 64), 64)
         c, s = cos_ref[at, :], sin_ref[at, :]
         dc, ds = dcos_ref[at, :], dsin_ref[at, :]
-        sign = sign_ref[at, :].astype(jnp.bfloat16)
-        out = (step >> 2) * (2 * OWNERS) + (step & 3) * 64
-        re = pl.ds(pl.multiple_of(out, 64), 64)
-        im = pl.ds(pl.multiple_of(out + OWNERS, 64), 64)
-        half = FRAME // 256
-        for v in range(half):
-            cb, sb = c.astype(jnp.bfloat16), (-s).astype(jnp.bfloat16)
-            table_ref[re, v * 128 : (v + 1) * 128] = cb
-            table_ref[im, v * 128 : (v + 1) * 128] = sb
-            table_ref[re, (v + half) * 128 : (v + half + 1) * 128] = cb * sign
-            table_ref[im, (v + half) * 128 : (v + half + 1) * 128] = sb * sign
-            if v < half - 1:
+        for v in range(FRAME // 256):
+            table_ref[0, at, v * 128 : (v + 1) * 128] = c.astype(jnp.bfloat16)
+            table_ref[1, at, v * 128 : (v + 1) * 128] = (-s).astype(jnp.bfloat16)
+            if v < FRAME // 256 - 1:
                 c, s = dc * c - ds * s, ds * c + dc * s
         return carry
 
     lax.fori_loop(0, LIVE // 64, turn, 0)
 
 
-def late_kernel(volt_ref, window_ref, _, late_ref):
-    def lanes(b, carry):
-        lane = pl.multiple_of(b * 128, 128)
-
-        def load(f, rows):
-            return volt_ref[rows : rows + 16, pl.ds(pl.multiple_of(f * FRAME + lane, 128), 128)]
-
-        def store(f, rows, value):
-            at = (f - EARLY) * IN_DEV + rows
-            late_ref[at : at + 16, pl.ds(lane, 128)] = value
-
-        filter_block(window_ref, load, store, range(EARLY, FR_DEV), lane)
-        return carry
-
-    lax.fori_loop(0, FRAME // 128, lanes, 0)
+def late_kernel(volt_ref, window_ref, _, even_ref, odd_ref, middle_ref, last_ref):
+    def load(f, rows, lane):
+        return volt_ref[rows : rows + 16, pl.ds(pl.multiple_of(f * FRAME + lane, 128), 128)]
+
+    fold_frames(window_ref, load, range(EARLY, FR_DEV), even_ref, odd_ref, middle_ref, last_ref)
 
 
 def transposed_dot(a, b):
     return lax.dot_general(a, b, (((1,), (1,)), ((), ())), preferred_element_type=jnp.float32)
 
 
-def spectra_kernel(halo_ref, volt_ref, window_ref, table_ref, late_ref, out_ref, early_ref, wide_ref):
-    @pl.when(pl.program_id(0) == 0)
+def put_spectra(table, sign, even, odd, middle, wide_ref, first):
+    real = transposed_dot(table[0], even) + transposed_dot(sign, middle)
+    for r, value in enumerate((real, transposed_dot(table[1], odd))):
+        for h in range(2):
+            wide_ref[pl.ds(r * PAIRS + first + h, OWNERS, 2 * PAIRS), :] = value[:, h * 128 : (h + 1) * 128]
+
+
+def late_spectra_kernel(table_ref, sign_ref, even_ref, odd_ref, middle_ref, wide_ref):
+    for c in range(LIVE_DEV):
+        at = slice(c * OWNERS, (c + 1) * OWNERS)
+        for n in range(PAIRS // 2 - 1):
+            rows = slice(n * 256, (n + 1) * 256)
+            table = table_ref[0, at, :], table_ref[1, at, :]
+            sources = even_ref[rows, :], odd_ref[rows, :], middle_ref[rows, :]
+            put_spectra(table, sign_ref[at, :], *sources, wide_ref.at[c], 2 * (n + 1))
+
+
+def spectra_kernel(
+    halo_ref, volt_ref, window_ref, table_ref, sign_ref, late_ref, out_ref, even_ref, odd_ref, middle_ref, last_ref, wide_ref
+):
+    c = pl.program_id(0)
+
+    @pl.when(c == 0)
     def _():
-        def lanes(b, carry):
-            lane = pl.multiple_of(b * 128, 128)
-
-            def load(f, rows):
-                ref, g = (halo_ref, f + TAPS - 1) if f < 0 else (volt_ref, f)
-                return ref[rows : rows + 16, pl.ds(pl.multiple_of(g * FRAME + lane, 128), 128)]
-
-            def store(f, rows, value):
-                at = f * IN_DEV + rows
-                early_ref[at : at + 16, pl.ds(lane, 128)] = value
-
-            filter_block(window_ref, load, store, range(EARLY), lane)
-            return carry
-
-        lax.fori_loop(0, FRAME // 128, lanes, 0)
-
-    table = table_ref[pl.ds(pl.multiple_of(pl.program_id(0) * 2 * OWNERS, 2 * OWNERS), 2 * OWNERS), :]
-    for n in range(PAIRS // 2):
-        block = early_ref[...] if n == 0 else late_ref[(n - 1) * 256 : n * 256, :]
-        both = transposed_dot(table, block)
-        for r in range(2):
-            for h in range(2):
-                value = both[r * OWNERS : (r + 1) * OWNERS, h * 128 : (h + 1) * 128]
-                wide_ref[pl.ds(r * PAIRS + 2 * n + h, OWNERS, 2 * PAIRS), :] = value
-    out_ref[...] = wide_ref[...].reshape(OWNERS, 2 * PAIRS, 128).astype(jnp.bfloat16)
+        def load(f, rows, lane):
+            ref, g = (halo_ref, f + TAPS - 1) if f < 0 else (volt_ref, f)
+            return ref[rows : rows + 16, pl.ds(pl.multiple_of(g * FRAME + lane, 128), 128)]
+
+        fold_frames(window_ref, load, range(EARLY), even_ref, odd_ref, middle_ref, last_ref)
+
+    at = pl.ds(pl.multiple_of(c * OWNERS, OWNERS), OWNERS)
+    table = table_ref[0, at, :], table_ref[1, at, :]
+    put_spectra(table, sign_ref[at, :], even_ref[...], odd_ref[...], middle_ref[...], wide_ref, 0)
+
+    def join(step, carry):
+        rows = pl.ds(pl.multiple_of(step * 256, 256), 256)
+        early = lax.broadcasted_iota(jnp.int32, (256, 128), 0) & (PAIRS - 1) < EARLY // 2
+        value = jnp.where(early, wide_ref[rows, :], late_ref[c, rows, :])
+        owners = pl.ds(pl.multiple_of(step * 16, 16), 16)
+        out_ref[owners] = value.reshape(16, 2 * PAIRS, 128).astype(jnp.bfloat16)
+        return carry
+
+    lax.fori_loop(0, OWNERS // 16, join, 0)
 
 
 def beam_kernel(recv_ref, slot_ref, position_ref, sub_ref, out_ref, x_ref, place_ref, cell_ref, part_ref, beam_ref):
@@ -268,42 +282,54 @@
     late_rows = (FR_DEV - EARLY) * IN_DEV
     early_rows = EARLY * IN_DEV
     params = pltpu.CompilerParams(vmem_limit_bytes=32 * MIB)
-    table = pl.pallas_call(
+    half = FRAME // 2
+    table, sign = pl.pallas_call(
         table_kernel,
         name="channel_table",
-        out_shape=jax.ShapeDtypeStruct((2 * LIVE, FRAME), bf16),
-        scratch_shapes=[pltpu.VMEM((LIVE, 128), f32)] * 5,
+        out_shape=[jax.ShapeDtypeStruct((2, LIVE, half), bf16), jax.ShapeDtypeStruct((LIVE, 128), bf16)],
+        scratch_shapes=[pltpu.VMEM((LIVE, 128), f32)] * 4,
         compiler_params=params,
-        cost_estimate=cost(4e9, 6 * MIB),
+        cost_estimate=cost(4e9, 3 * MIB),
     )(channel_flags.reshape(CHANNELS // 128, 128))
-    late = pl.pallas_call(
+    folded = pl.pallas_call(
         late_kernel,
         name="filter",
         in_specs=[in_vmem, in_vmem, pl.BlockSpec(memory_space=pl.ANY)],
-        out_shape=jax.ShapeDtypeStruct((late_rows, FRAME), bf16),
+        out_shape=[
+            jax.ShapeDtypeStruct((late_rows, half), bf16),
+            jax.ShapeDtypeStruct((late_rows, half), bf16),
+            jax.ShapeDtypeStruct((late_rows, 128), bf16),
+        ],
+        scratch_shapes=[pltpu.VMEM((late_rows, 128), f32)],
         compiler_params=params,
         cost_estimate=cost(4e9, 7 * MIB),
     )(voltages, window, table)
+    late = pl.pallas_call(
+        late_spectra_kernel,
+        name="late_spectra",
+        in_specs=[in_vmem] * 5,
+        out_specs=in_vmem,
+        out_shape=jax.ShapeDtypeStruct((LIVE_DEV, OWNERS * 2 * PAIRS, 128), f32),
+        compiler_params=params,
+        cost_estimate=cost(4e9, 12 * MIB),
+    )(table, sign, *folded)
     sent = pl.pallas_call(
         spectra_kernel,
         name="spectra",
         grid=(LIVE_DEV,),
-        in_specs=[
-            in_vmem,
-            whole((IN_DEV, EARLY * FRAME)),
-            in_vmem,
-            in_vmem,
-            in_vmem,
-        ],
+        in_specs=[in_vmem, whole((IN_DEV, EARLY * FRAME)), in_vmem, in_vmem, in_vmem, in_vmem],
         out_specs=pl.BlockSpec((OWNERS, 2 * PAIRS, 128), lambda c: (0, c, 0)),
         out_shape=pltpu.HBM((OWNERS, LIVE_DEV * 2 * PAIRS, 128), bf16),
         scratch_shapes=[
-            pltpu.VMEM((early_rows, FRAME), bf16),
+            pltpu.VMEM((early_rows, half), bf16),
+            pltpu.VMEM((early_rows, half), bf16),
+            pltpu.VMEM((early_rows, 128), bf16),
+            pltpu.VMEM((early_rows, 128), f32),
             pltpu.VMEM((OWNERS * 2 * PAIRS, 128), f32),
         ],
         compiler_params=params,
-        cost_estimate=cost(7e9, 14 * MIB),
-    )(halo, voltages, window, table, late)
+        cost_estimate=cost(2e9, 14 * MIB),
+    )(halo, voltages, window, table, sign, late)
     got = lax.all_to_all(sent, ("feed", "tm"), split_axis=0, concat_axis=0, tiled=True)
     inputs = N_FEED * IN_DEV
     rows = LIVE_DEV * 256

time: 129 us -> 125 us (0.969)
  Pallas kernels: 30.9 us -> 28.3 us
  blocking collectives: 90.7 us -> 89.2 us
    pallas_call x1, Pallas kernels: 10.3 us -> 5.12 us  [local(): pl.pallas_call(spectra_kernel, name='spectra', grid=(LIVE_DEV,), in_specs...]
    pallas_call x1 -> x2, Pallas kernels: 5.4 us -> 7.61 us  [the longest x1 4.05 us: local(): pl.pallas_call(table_kernel, name='channel_table', out_shape=[jax.ShapeDt...]
    all_to_all x1, blocking collectives: 90.7 us -> 89.2 us  [local(): lax.all_to_all(sent, ('feed', 'tm'), split_axis=0, concat_axis=0, tiled=T...]
  transfers between devices with their start and end apart: 1 -> 1, of which waited for: 1 -> 0; matrix products, arithmetic and copies ran while one was open for 0% -> 0% of each run, Pallas kernels for 6% -> 8%
where the time goes in v3:
time: 125 us; the launch traced here: 124 us
  blocking collectives  89.2 us (71%)
  Pallas kernels  28.3 us (23%)
  starting transfers between devices  4.59 us (4%)
  local copies, waits for them, and re-layouts  2.21 us (2%)
    all_to_all x1, blocking collectives, local(): lax.all_to_all(sent, ('feed', 'tm'), split_axis=0, concat_axis=0, tiled=T...  89.2 us
    pallas_call x1, Pallas kernels, local(): pl.pallas_call(beam_kernel, name='beams_and_power', in_specs=[in_vmem] *...  13.2 us
    pallas_call x1, Pallas kernels, local(): pl.pallas_call(spectra_kernel, name='spectra', grid=(LIVE_DEV,), in_specs...  5.12 us
    ppermute x1, starting transfers between devices, local(): halo = lax.ppermute(history, 'tm', [(i, i + 1) for i in range(N_TM - 1)])  4.59 us
    pallas_call x1, Pallas kernels, local(): pl.pallas_call(table_kernel, name='channel_table', out_shape=[jax.ShapeDt...  4.05 us
    pallas_call x1, Pallas kernels, local(): pl.pallas_call(late_spectra_kernel, name='late_spectra', in_specs=[in_vme...  3.56 us
  transfers between devices with their start and end apart: 1, of which 0 were waited for; matrix products, arithmetic and copies ran while one was open for 0% of the time, Pallas kernels for 8%

profile of v3, /device:TPU:1, one launch (start us, length us, event | category | flops | bytes accessed | tf_op | source)
XLA Modules:
  0.0 124.4 jit_solution(13428854126742808421)
XLA Ops:
  0.0 1.2 slice.3
  1.2 4.6 %collective-permute-start = (bf16[64,6144]{1,0:T(8,128)(2,1)S(1)}, bf16[64,6144]{1,0:T(8,128)(2,1)S(1)}, u32[]{:S(2)}, u32[]{:S(2)}) collective-permute-start(bf16[64,6144]{1,0:T(8,128)(2,1)S(1)} %slice.3), channel_id=1, source_target_pairs={{0,1},{1,2},{2,3},{3,4},{4,5},{5,6},{6,7},{8,9},{9,10},{10,11},{11... | collective-permute-start | bytes 2359304 | tf_op jit(solution)/shard_map/ppermute | solution.py:279
  5.8 0.0 copy-start.2
  5.8 0.7 copy-done.2
  6.5 0.0 copy-start
  6.5 0.0 copy-start.1
  6.5 4.1 %channel_table.1 = (bf16[2,768,1024]{2,1,0:T(8,128)(2,1)S(1)}, bf16[768,128]{1,0:T(8,128)(2,1)S(1)}) custom-call(s32[8,128]{1,0:T(8,128)S(1)} %bitcast.1), custom_call_target="tpu_custom_call" | custom-call | flops 4000000000 | bytes 3145728 | tf_op jit(solution)/shard_map/channel_table/pallas_call | solution.py:286
  10.5 0.0 copy-done
  10.6 0.0 copy-done.1
  10.6 2.4 %filter.1 = (bf16[768,1024]{1,0:T(8,128)(2,1)S(1)}, bf16[768,1024]{1,0:T(8,128)(2,1)S(1)}, bf16[768,128]{1,0:T(8,128)(2,1)S(1)}) custom-call(bf16[64,32768]{1,0:T(8,128)(2,1)S(1)} %copy-done, f32[4,2048]{1,0:T(4,128)S(1)} %copy-done.1, bf16[2,768,1024]{2,1,0:T(8,128)(2,1)S(1)} %get-tuple-element.10._.table_ref), custom_call_target="tpu_custom_call" | custom-call | flops 4000000000 | bytes 7340032 | tf_op jit(solution)/shard_map/filter/pallas_call | solution.py:294
  13.0 3.6 %late_spectra.1.late_ref = f32[3,4096,128]{2,1,0:T(8,128)S(1)} custom-call(bf16[2,768,1024]{2,1,0:T(8,128)(2,1)S(1)} %get-tuple-element.10._.table_ref, bf16[768,128]{1,0:T(8,128)(2,1)S(1)} %get-tuple-element.11.sign_ref, bf16[768,1024]{1,0:T(8,128)(2,1)S(1)} %get-tuple-element.12.even_ref, bf16[768,1024]{1,0:T(8,128)(2,1)S(1)} %get-tuple-element.13.odd_ref, ...), custom_call_target="tpu_custom_call" | custom-call | flops 4000000000 | bytes 12582912 | tf_op jit(solution)/shard_map/late_spectra/pallas_call | solution.py:307
  16.6 0.0 collective-permute-done.halo_ref
  16.6 5.1 %spectra.1 = bf16[256,48,128]{2,1,0:T(8,128)(2,1)} custom-call(bf16[64,6144]{1,0:T(8,128)(2,1)S(1)} %collective-permute-done.halo_ref, bf16[64,32768]{1,0:T(8,128)(2,1)S(1)} %copy-done, f32[4,2048]{1,0:T(4,128)S(1)} %copy-done.1, bf16[2,768,1024]{2,1,0:T(8,128)(2,1)S(1)} %get-tuple-element.10._.table_ref, bf16[768,128]{1,0:T(8,128)(2,1)S(1)} %get-tuple-element.11.sign_ref, ...), custom_call_target="tpu_custom_call" | custom-call | flops 2000000000 | bytes 14680064 | tf_op jit(solution)/shard_map/spectra/pallas_call | solution.py:316
  21.7 0.0 copy-start.5
  21.7 0.0 copy-start.3
  21.7 0.0 copy-start.4
  21.7 89.2 %all_to_all.5.recv_ref = bf16[256,48,128]{2,1,0:T(8,128)(2,1)S(1)} all-to-all(bf16[256,48,128]{2,1,0:T(8,128)(2,1)} %spectra.1), channel_id=1, replica_groups=mesh['feed'=32,'tm'=8] {'feed','tm'}, dimensions={0} | all-to-all | bytes 6291456 | tf_op jit(solution)/shard_map/all_to_all | solution.py:333
  110.9 0.0 copy-done.5
  110.9 0.3 broadcast_in_dim.2.slot_ref
  111.2 0.0 copy-done.3
  111.2 0.0 copy-done.4
  111.2 13.2 %beams_and_power.1 = f32[3,16,1024]{2,1,0:T(8,128)} custom-call(bf16[256,48,128]{2,1,0:T(8,128)(2,1)S(1)} %all_to_all.5.recv_ref, s32[2048,128]{1,0:T(8,128)S(1)} %broadcast_in_dim.2.slot_ref, bf16[512,512]{1,0:T(8,128)(2,1)S(1)} %copy-done.3, bf16[256,256]{1,0:T(8,128)(2,1)S(1)} %copy-done.4), custom_call_target="tpu_custom_call" | custom-call | flops 8999999488 | bytes 6291456 | tf_op jit(solution)/shard_map/beams_and_power/pallas_call | solution.py:336
Async XLA Ops:
  1.2 15.4 %collective-permute-start = (bf16[64,6144]{1,0:T(8,128)(2,1)S(1)}, bf16[64,6144]{1,0:T(8,128)(2,1)S(1)}, u32[]{:S(2)}, u32[]{:S(2)}) collective-permute-start(bf16[64,6144]{1,0:T(8,128)(2,1)S(1)} %slice.3), channel_id=1, source_target_pairs={{0,1},{1,2},{2,3},{3,4},{4,5},{5,6},{6,7},{8,9},{9,10},{10,11},{11... | collective-permute-start | bytes 2359304 | tf_op jit(solution)/shard_map/ppermute | solution.py:279
  5.8 0.7 copy-start.2
  6.5 4.1 %copy-start = (bf16[64,32768]{1,0:T(8,128)(2,1)S(1)}, bf16[64,32768]{1,0:T(8,128)(2,1)}, u32[]{:S(2)}) copy-start(bf16[64,32768]{1,0:T(8,128)(2,1)} %volt_ref.3) | copy-start | bytes 12582916
  6.5 4.1 %copy-start.1 = (f32[4,2048]{1,0:T(4,128)S(1)}, f32[4,2048]{1,0:T(4,128)}, u32[]{:S(2)}) copy-start(f32[4,2048]{1,0:T(4,128)} %constant.6.clone.window_ref) | copy-start | bytes 98308
  21.7 89.2 %copy-start.5 = (s32[2048]{0:T(1024)S(1)}, s32[2048]{0:T(1024)}, u32[]{:S(2)}) copy-start(s32[2048]{0:T(1024)} %param.7) | copy-start | bytes 24580
  21.7 89.5 %copy-start.3 = (bf16[512,512]{1,0:T(8,128)(2,1)S(1)}, bf16[512,512]{1,0:T(8,128)(2,1)}, u32[]{:S(2)}) copy-start(bf16[512,512]{1,0:T(8,128)(2,1)} %constant.7.clone.position_ref) | copy-start | bytes 1572868
  21.7 89.5 %copy-start.4 = (bf16[256,256]{1,0:T(8,128)(2,1)S(1)}, bf16[256,256]{1,0:T(8,128)(2,1)}, u32[]{:S(2)}) copy-start(bf16[256,256]{1,0:T(8,128)(2,1)} %constant.8.clone.sub_ref) | copy-start | bytes 393220

commit v4 on v3

--- a/solution.py
+++ b/solution.py
@@ -71,6 +71,7 @@
 def fold_frames(window_ref, load, frames, even_ref, odd_ref, middle_ref, last_ref):
     lane = lax.broadcasted_iota(jnp.int32, (16, 128), 1)
     back = (128 - lane) & 127
+    swap = lax.axis_index("feed") & 1
     last_ref[...] = jnp.zeros_like(last_ref)
 
     def piece(v, carry):
@@ -87,7 +88,7 @@
                             held[j][g] = load(g, rows, sides[j]).astype(jnp.float32)
                         term = taps[j][t] * held[j][g]
                         total[j] = term if t == 0 else total[j] + term
-                at = slice(n * IN_DEV + rows, n * IN_DEV + rows + 16)
+                at = pl.ds(pl.multiple_of((n ^ swap) * IN_DEV + rows, 16), 16)
                 turned = jnp.take_along_axis(total[1], back, axis=1, mode="promise_in_bounds")
                 mirror = jnp.where(lane == 0, last_ref[at, :], turned)
                 last_ref[at, :] = turned
@@ -99,7 +100,7 @@
     lax.fori_loop(0, FRAME // 256, piece, 0)
 
 
-def table_kernel(flags_ref, table_ref, sign_ref, cos_ref, sin_ref, dcos_ref, dsin_ref):
+def table_kernel(flags_ref, table_ref, sign_ref, below_ref, channel_ref):
     lane = lax.broadcasted_iota(jnp.int32, (64, 128), 1)
     upto = (lax.broadcasted_iota(jnp.int32, (128, 128), 0) <= lax.broadcasted_iota(jnp.int32, (128, 128), 1)).astype(
         jnp.float32
@@ -116,29 +117,25 @@
         counts.append((count[r : r + 1, :128] + earlier).astype(jnp.int32))
         earlier = earlier + count[r : r + 1, 128:]
 
-    def place(step, carry):
+    def ranks(step, carry):
         row = lax.broadcasted_iota(jnp.int32, (64, 128), 0) + step * 64
         rank = (row & (OWNERS - 1)) * LIVE_DEV + (row >> 8)
-        below = sum((c <= rank).astype(jnp.float32) for c in counts).astype(jnp.bfloat16)
-        channel = jnp.dot(below, ones, preferred_element_type=jnp.float32).astype(jnp.int32)
         at = pl.ds(pl.multiple_of(step * 64, 64), 64)
+        below_ref[at, :] = sum((c <= rank).astype(jnp.float32) for c in counts).astype(jnp.bfloat16)
+        return carry
+
+    lax.fori_loop(0, LIVE // 64, ranks, 0)
+    channel_ref[...] = jnp.dot(below_ref[...], ones, preferred_element_type=jnp.float32)
+
+    def turn(step, carry):
+        at = pl.ds(pl.multiple_of(step * 64, 64), 64)
+        channel = channel_ref[at, :].astype(jnp.int32)
+        scale = np.float32(1.0 / math.sqrt(FRAME))
         c, s = unit_circle((channel * lane) & (FRAME - 1))
-        scale = np.float32(1.0 / math.sqrt(FRAME))
-        cos_ref[at, :] = c * scale
-        sin_ref[at, :] = s * scale
-        c, s = unit_circle((channel * 128) & (FRAME - 1))
-        dcos_ref[at, :] = c
-        dsin_ref[at, :] = s
+        c, s = c * scale, s * scale
+        dc, ds = unit_circle((channel * 128) & (FRAME - 1))
         sign = (1 - 2 * (channel & 1)).astype(jnp.float32) * scale
         sign_ref[at, :] = jnp.where(lane == 0, sign, 0.0).astype(jnp.bfloat16)
-        return carry
-
-    lax.fori_loop(0, LIVE // 64, place, 0)
-
-    def turn(step, carry):
-        at = pl.ds(pl.multiple_of(step * 64, 64), 64)
-        c, s = cos_ref[at, :], sin_ref[at, :]
-        dc, ds = dcos_ref[at, :], dsin_ref[at, :]
         for v in range(FRAME // 256):
             table_ref[0, at, v * 128 : (v + 1) * 128] = c.astype(jnp.bfloat16)
             table_ref[1, at, v * 128 : (v + 1) * 128] = (-s).astype(jnp.bfloat16)
@@ -216,8 +213,8 @@
                 part = slice(c * 2 * PAIRS, (c + 1) * 2 * PAIRS)
                 one = recv_ref[2 * s * N_TM + b, part].astype(jnp.float32)
                 two = recv_ref[(2 * s + 1) * N_TM + b, part].astype(jnp.float32)
-                even = jnp.where(low, one, pltpu.roll(two, 64, 1))
-                odd = jnp.where(low, pltpu.roll(one, 64, 1), two)
+                even = jnp.where(low, one, two)
+                odd = pltpu.roll(jnp.where(low, two, one), 64, 1)
                 row = c * 256 + b * 32
                 x_ref[row : row + 16, pl.ds(lane, 128)] = even.astype(jnp.bfloat16)
                 x_ref[row + 16 : row + 32, pl.ds(lane, 128)] = odd.astype(jnp.bfloat16)
@@ -232,12 +229,11 @@
         cells = cells.reshape(-1, 2, PAIRS, NS)
         both = [cells[:, r].reshape(-1, NS) for r in range(2)]
         cell_ref[i] = jnp.concatenate(both, axis=1).astype(jnp.bfloat16)
-    for i in range(groups):
-        part_ref[i] = jnp.dot(cell_ref[i], position_ref[...], preferred_element_type=jnp.float32)
     for p in range(2):
-
-        def join(f, carry):
-            rows = pl.ds(pl.multiple_of(f * PAIRS, PAIRS), PAIRS)
+        for i in range(p * CYL, (p + 1) * CYL):
+            part_ref[i] = jnp.dot(cell_ref[i], position_ref[...], preferred_element_type=jnp.float32)
+        for f in range(LIVE_DEV * 16):
+            rows = slice(f * PAIRS, (f + 1) * PAIRS)
             re = [part_ref[p * CYL + y, rows, :NS] for y in range(CYL)]
             im = [part_ref[p * CYL + y, rows, NS:] for y in range(CYL)]
             re_s, re_d = re[0] + re[2], re[0] - re[2]
@@ -246,13 +242,10 @@
             im_t, im_e = im[1] + im[3], im[1] - im[3]
             out_re = [re_s + re_t, re_d + im_e, re_s - re_t, re_d - im_e]
             out_im = [im_s + im_t, im_d - re_e, im_s - im_t, im_d + re_e]
-            at = pl.ds(pl.multiple_of(f * 2 * PAIRS, 2 * PAIRS), 2 * PAIRS)
+            at = slice(f * 2 * PAIRS, (f + 1) * 2 * PAIRS)
             for e in range(CYL):
                 value = jnp.concatenate([out_re[e], out_im[e]], axis=0) * 0.5
                 beam_ref[p, at, e * NS : (e + 1) * NS] = value.astype(jnp.bfloat16)
-            return carry
-
-        lax.fori_loop(0, LIVE_DEV * 16, join, 0, unroll=2)
     for c in range(LIVE_DEV):
         for e in range(CYL):
             total = None
@@ -287,7 +280,7 @@
         table_kernel,
         name="channel_table",
         out_shape=[jax.ShapeDtypeStruct((2, LIVE, half), bf16), jax.ShapeDtypeStruct((LIVE, 128), bf16)],
-        scratch_shapes=[pltpu.VMEM((LIVE, 128), f32)] * 4,
+        scratch_shapes=[pltpu.VMEM((LIVE, 128), bf16), pltpu.VMEM((LIVE, 128), f32)],
         compiler_params=params,
         cost_estimate=cost(4e9, 3 * MIB),
     )(channel_flags.reshape(CHANNELS // 128, 128))
@@ -317,7 +310,7 @@
         spectra_kernel,
         name="spectra",
         grid=(LIVE_DEV,),
-        in_specs=[in_vmem, whole((IN_DEV, EARLY * FRAME)), in_vmem, in_vmem, in_vmem, in_vmem],
+        in_specs=[in_vmem] * 6,
         out_specs=pl.BlockSpec((OWNERS, 2 * PAIRS, 128), lambda c: (0, c, 0)),
         out_shape=pltpu.HBM((OWNERS, LIVE_DEV * 2 * PAIRS, 128), bf16),
         scratch_shapes=[

time: 125 us -> 123 us (0.984)
  Pallas kernels: 28.3 us -> 26.3 us
    pallas_call x1, Pallas kernels: 13.2 us -> 11.8 us  [local(): pl.pallas_call(beam_kernel, name='beams_and_power', in_specs=[in_vmem] *...]
  transfers between devices with their start and end apart: 1 -> 1, of which waited for: 0 -> 0; matrix products, arithmetic and copies ran while one was open for 0% -> 0% of each run, Pallas kernels for 8% -> 7%
where the time goes in v4:
time: 123 us
  blocking collectives  89.6 us (73%)
  Pallas kernels  26.3 us (21%)
  starting transfers between devices  4.59 us (4%)
  local copies, waits for them, and re-layouts  2.21 us (2%)
    all_to_all x1, blocking collectives, local(): lax.all_to_all(sent, ('feed', 'tm'), split_axis=0, concat_axis=0, tiled=T...  89.6 us
    pallas_call x1, Pallas kernels, local(): pl.pallas_call(beam_kernel, name='beams_and_power', in_specs=[in_vmem] *...  11.8 us
    pallas_call x1, Pallas kernels, local(): pl.pallas_call(spectra_kernel, name='spectra', grid=(LIVE_DEV,), in_specs...  5.3 us
    ppermute x1, starting transfers between devices, local(): halo = lax.ppermute(history, 'tm', [(i, i + 1) for i in range(N_TM - 1)])  4.59 us
    pallas_call x1, Pallas kernels, local(): pl.pallas_call(late_spectra_kernel, name='late_spectra', in_specs=[in_vme...  3.56 us
    pallas_call x1, Pallas kernels, local(): pl.pallas_call(table_kernel, name='channel_table', out_shape=[jax.ShapeDt...  2.85 us
    pallas_call x1, Pallas kernels, local(): pl.pallas_call(late_kernel, name='filter', in_specs=[in_vmem, in_vmem, pl...  2.79 us
  transfers between devices with their start and end apart: 1, of which 0 were waited for; matrix products, arithmetic and copies ran while one was open for 0% of the time, Pallas kernels for 7%

profile of v4, /device:TPU:1, one launch (start us, length us, event | category | flops | bytes accessed | tf_op | source)
XLA Modules:
  0.0 122.8 jit_solution(11935766491590867377)
XLA Ops:
  0.0 1.2 slice.3
  1.2 4.6 %collective-permute-start = (bf16[64,6144]{1,0:T(8,128)(2,1)S(1)}, bf16[64,6144]{1,0:T(8,128)(2,1)S(1)}, u32[]{:S(2)}, u32[]{:S(2)}) collective-permute-start(bf16[64,6144]{1,0:T(8,128)(2,1)S(1)} %slice.3), channel_id=1, source_target_pairs={{0,1},{1,2},{2,3},{3,4},{4,5},{5,6},{6,7},{8,9},{9,10},{10,11},{11... | collective-permute-start | bytes 2359304 | tf_op jit(solution)/shard_map/ppermute | solution.py:272
  5.8 0.0 copy-start.2
  5.8 0.7 copy-done.2
  6.5 0.0 copy-start
  6.5 0.0 copy-start.1
  6.5 2.8 %channel_table.1 = (bf16[2,768,1024]{2,1,0:T(8,128)(2,1)S(1)}, bf16[768,128]{1,0:T(8,128)(2,1)S(1)}) custom-call(s32[8,128]{1,0:T(8,128)S(1)} %bitcast.1), custom_call_target="tpu_custom_call" | custom-call | flops 4000000000 | bytes 3145728 | tf_op jit(solution)/shard_map/channel_table/pallas_call | solution.py:279
  9.3 0.0 copy-done
  9.4 0.0 copy-done.1
  9.4 2.8 %filter.1 = (bf16[768,1024]{1,0:T(8,128)(2,1)S(1)}, bf16[768,1024]{1,0:T(8,128)(2,1)S(1)}, bf16[768,128]{1,0:T(8,128)(2,1)S(1)}) custom-call(bf16[64,32768]{1,0:T(8,128)(2,1)S(1)} %copy-done, f32[4,2048]{1,0:T(4,128)S(1)} %copy-done.1, bf16[2,768,1024]{2,1,0:T(8,128)(2,1)S(1)} %get-tuple-element.10._.table_ref), custom_call_target="tpu_custom_call" | custom-call | flops 4000000000 | bytes 7340032 | tf_op jit(solution)/shard_map/filter/pallas_call | solution.py:287
  12.2 3.6 %late_spectra.1.late_ref = f32[3,4096,128]{2,1,0:T(8,128)S(1)} custom-call(bf16[2,768,1024]{2,1,0:T(8,128)(2,1)S(1)} %get-tuple-element.10._.table_ref, bf16[768,128]{1,0:T(8,128)(2,1)S(1)} %get-tuple-element.11.sign_ref, bf16[768,1024]{1,0:T(8,128)(2,1)S(1)} %get-tuple-element.12.even_ref, bf16[768,1024]{1,0:T(8,128)(2,1)S(1)} %get-tuple-element.13.odd_ref, ...), custom_call_target="tpu_custom_call" | custom-call | flops 4000000000 | bytes 12582912 | tf_op jit(solution)/shard_map/late_spectra/pallas_call | solution.py:300
  15.7 0.0 collective-permute-done.halo_ref
  15.7 5.3 %spectra.1 = bf16[256,48,128]{2,1,0:T(8,128)(2,1)} custom-call(bf16[64,6144]{1,0:T(8,128)(2,1)S(1)} %collective-permute-done.halo_ref, bf16[64,32768]{1,0:T(8,128)(2,1)S(1)} %copy-done, f32[4,2048]{1,0:T(4,128)S(1)} %copy-done.1, bf16[2,768,1024]{2,1,0:T(8,128)(2,1)S(1)} %get-tuple-element.10._.table_ref, bf16[768,128]{1,0:T(8,128)(2,1)S(1)} %get-tuple-element.11.sign_ref, ...), custom_call_target="tpu_custom_call" | custom-call | flops 2000000000 | bytes 14680064 | tf_op jit(solution)/shard_map/spectra/pallas_call | solution.py:309
  21.0 0.0 copy-start.5
  21.0 0.0 copy-start.3
  21.0 0.0 copy-start.4
  21.0 89.6 %all_to_all.5.recv_ref = bf16[256,48,128]{2,1,0:T(8,128)(2,1)S(1)} all-to-all(bf16[256,48,128]{2,1,0:T(8,128)(2,1)} %spectra.1), channel_id=1, replica_groups=mesh['feed'=32,'tm'=8] {'feed','tm'}, dimensions={0} | all-to-all | bytes 6291456 | tf_op jit(solution)/shard_map/all_to_all | solution.py:326
  110.6 0.0 copy-done.5
  110.6 0.3 broadcast_in_dim.2.slot_ref
  110.9 0.0 copy-done.3
  111.0 0.0 copy-done.4
  111.0 11.8 %beams_and_power.1 = f32[3,16,1024]{2,1,0:T(8,128)} custom-call(bf16[256,48,128]{2,1,0:T(8,128)(2,1)S(1)} %all_to_all.5.recv_ref, s32[2048,128]{1,0:T(8,128)S(1)} %broadcast_in_dim.2.slot_ref, bf16[512,512]{1,0:T(8,128)(2,1)S(1)} %copy-done.3, bf16[256,256]{1,0:T(8,128)(2,1)S(1)} %copy-done.4), custom_call_target="tpu_custom_call" | custom-call | flops 8999999488 | bytes 6291456 | tf_op jit(solution)/shard_map/beams_and_power/pallas_call | solution.py:329
Async XLA Ops:
  1.2 14.5 %collective-permute-start = (bf16[64,6144]{1,0:T(8,128)(2,1)S(1)}, bf16[64,6144]{1,0:T(8,128)(2,1)S(1)}, u32[]{:S(2)}, u32[]{:S(2)}) collective-permute-start(bf16[64,6144]{1,0:T(8,128)(2,1)S(1)} %slice.3), channel_id=1, source_target_pairs={{0,1},{1,2},{2,3},{3,4},{4,5},{5,6},{6,7},{8,9},{9,10},{10,11},{11... | collective-permute-start | bytes 2359304 | tf_op jit(solution)/shard_map/ppermute | solution.py:272
  5.8 0.7 copy-start.2
  6.5 2.9 %copy-start = (bf16[64,32768]{1,0:T(8,128)(2,1)S(1)}, bf16[64,32768]{1,0:T(8,128)(2,1)}, u32[]{:S(2)}) copy-start(bf16[64,32768]{1,0:T(8,128)(2,1)} %volt_ref.3) | copy-start | bytes 12582916
  6.5 2.9 %copy-start.1 = (f32[4,2048]{1,0:T(4,128)S(1)}, f32[4,2048]{1,0:T(4,128)}, u32[]{:S(2)}) copy-start(f32[4,2048]{1,0:T(4,128)} %constant.6.clone.window_ref) | copy-start | bytes 98308
  21.0 89.6 %copy-start.5 = (s32[2048]{0:T(1024)S(1)}, s32[2048]{0:T(1024)}, u32[]{:S(2)}) copy-start(s32[2048]{0:T(1024)} %param.7) | copy-start | bytes 24580
  21.0 89.9 %copy-start.3 = (bf16[512,512]{1,0:T(8,128)(2,1)S(1)}, bf16[512,512]{1,0:T(8,128)(2,1)}, u32[]{:S(2)}) copy-start(bf16[512,512]{1,0:T(8,128)(2,1)} %constant.7.clone.position_ref) | copy-start | bytes 1572868
  21.0 89.9 %copy-start.4 = (bf16[256,256]{1,0:T(8,128)(2,1)S(1)}, bf16[256,256]{1,0:T(8,128)(2,1)}, u32[]{:S(2)}) copy-start(bf16[256,256]{1,0:T(8,128)(2,1)} %constant.8.clone.sub_ref) | copy-start | bytes 393220

commit v5 on v4

--- a/solution.py
+++ b/solution.py
@@ -21,6 +21,7 @@
 LIVE_DEV = 3
 LIVE = 768
 OWNERS = 256
+OWNER_BLOCK = 64
 PAIRS = FR_DEV // 2
 EARLY = 4
 MIB = 1 << 20
@@ -68,10 +69,18 @@
     return cosine, sine
 
 
-def fold_frames(window_ref, load, frames, even_ref, odd_ref, middle_ref, last_ref):
+def fold_frames(*args):
+    odd = lax.axis_index("feed") & 1
+    for swap in range(2):
+
+        @pl.when(odd == swap)
+        def _():
+            fold_placed(swap, *args)
+
+
+def fold_placed(swap, window_ref, load, frames, even_ref, odd_ref, middle_ref, last_ref):
     lane = lax.broadcasted_iota(jnp.int32, (16, 128), 1)
     back = (128 - lane) & 127
-    swap = lax.axis_index("feed") & 1
     last_ref[...] = jnp.zeros_like(last_ref)
 
     def piece(v, carry):
@@ -88,7 +97,7 @@
                             held[j][g] = load(g, rows, sides[j]).astype(jnp.float32)
                         term = taps[j][t] * held[j][g]
                         total[j] = term if t == 0 else total[j] + term
-                at = pl.ds(pl.multiple_of((n ^ swap) * IN_DEV + rows, 16), 16)
+                at = slice((n ^ swap) * IN_DEV + rows, (n ^ swap) * IN_DEV + rows + 16)
                 turned = jnp.take_along_axis(total[1], back, axis=1, mode="promise_in_bounds")
                 mirror = jnp.where(lane == 0, last_ref[at, :], turned)
                 last_ref[at, :] = turned
@@ -157,49 +166,42 @@
     return lax.dot_general(a, b, (((1,), (1,)), ((), ())), preferred_element_type=jnp.float32)
 
 
-def put_spectra(table, sign, even, odd, middle, wide_ref, first):
-    real = transposed_dot(table[0], even) + transposed_dot(sign, middle)
-    for r, value in enumerate((real, transposed_dot(table[1], odd))):
-        for h in range(2):
-            wide_ref[pl.ds(r * PAIRS + first + h, OWNERS, 2 * PAIRS), :] = value[:, h * 128 : (h + 1) * 128]
+def put_spectra(table_ref, sign_ref, even, odd, middle, wide_ref, first):
+    real = transposed_dot(table_ref[0], even) + transposed_dot(sign_ref[...], middle)
+    for r, value in enumerate((real, transposed_dot(table_ref[1], odd))):
+        for c in range(LIVE_DEV):
+            for h in range(2):
+                part = value[c * OWNERS : (c + 1) * OWNERS, h * 128 : (h + 1) * 128]
+                wide_ref[c, pl.ds(r * PAIRS + first + h, OWNERS, 2 * PAIRS), :] = part
 
 
 def late_spectra_kernel(table_ref, sign_ref, even_ref, odd_ref, middle_ref, wide_ref):
-    for c in range(LIVE_DEV):
-        at = slice(c * OWNERS, (c + 1) * OWNERS)
-        for n in range(PAIRS // 2 - 1):
-            rows = slice(n * 256, (n + 1) * 256)
-            table = table_ref[0, at, :], table_ref[1, at, :]
-            sources = even_ref[rows, :], odd_ref[rows, :], middle_ref[rows, :]
-            put_spectra(table, sign_ref[at, :], *sources, wide_ref.at[c], 2 * (n + 1))
+    for n in range(PAIRS // 2 - 1):
+        rows = slice(n * 256, (n + 1) * 256)
+        put_spectra(table_ref, sign_ref, even_ref[rows, :], odd_ref[rows, :], middle_ref[rows, :], wide_ref, 2 * (n + 1))
 
 
 def spectra_kernel(
     halo_ref, volt_ref, window_ref, table_ref, sign_ref, late_ref, out_ref, even_ref, odd_ref, middle_ref, last_ref, wide_ref
 ):
-    c = pl.program_id(0)
-
-    @pl.when(c == 0)
+    step = pl.program_id(0)
+
+    @pl.when(step == 0)
     def _():
         def load(f, rows, lane):
             ref, g = (halo_ref, f + TAPS - 1) if f < 0 else (volt_ref, f)
             return ref[rows : rows + 16, pl.ds(pl.multiple_of(g * FRAME + lane, 128), 128)]
 
         fold_frames(window_ref, load, range(EARLY), even_ref, odd_ref, middle_ref, last_ref)
-
-    at = pl.ds(pl.multiple_of(c * OWNERS, OWNERS), OWNERS)
-    table = table_ref[0, at, :], table_ref[1, at, :]
-    put_spectra(table, sign_ref[at, :], even_ref[...], odd_ref[...], middle_ref[...], wide_ref, 0)
-
-    def join(step, carry):
-        rows = pl.ds(pl.multiple_of(step * 256, 256), 256)
-        early = lax.broadcasted_iota(jnp.int32, (256, 128), 0) & (PAIRS - 1) < EARLY // 2
-        value = jnp.where(early, wide_ref[rows, :], late_ref[c, rows, :])
-        owners = pl.ds(pl.multiple_of(step * 16, 16), 16)
-        out_ref[owners] = value.reshape(16, 2 * PAIRS, 128).astype(jnp.bfloat16)
-        return carry
-
-    lax.fori_loop(0, OWNERS // 16, join, 0)
+        put_spectra(table_ref, sign_ref, even_ref[...], odd_ref[...], middle_ref[...], wide_ref, 0)
+
+    size = OWNER_BLOCK * 2 * PAIRS
+    early = lax.broadcasted_iota(jnp.int32, (size, 128), 0) & (PAIRS - 1) < EARLY // 2
+    rows = pl.ds(pl.multiple_of(step * size, size), size)
+    for c in range(LIVE_DEV):
+        value = jnp.where(early, wide_ref[c, rows, :], late_ref[c, rows, :])
+        part = slice(c * 2 * PAIRS, (c + 1) * 2 * PAIRS)
+        out_ref[:, part, :] = value.reshape(OWNER_BLOCK, 2 * PAIRS, 128).astype(jnp.bfloat16)
 
 
 def beam_kernel(recv_ref, slot_ref, position_ref, sub_ref, out_ref, x_ref, place_ref, cell_ref, part_ref, beam_ref):
@@ -259,11 +261,6 @@
 
 def cost(flops, nbytes):
     return pl.CostEstimate(flops=int(flops), bytes_accessed=int(nbytes), transcendentals=0)
-
-
-def whole(shape, *index):
-    index = index or (0,) * len(shape)
-    return pl.BlockSpec(shape, lambda *_: index)
 
 
 def local(voltages, feed_slot, channel_flags):
@@ -309,16 +306,16 @@
     sent = pl.pallas_call(
         spectra_kernel,
         name="spectra",
-        grid=(LIVE_DEV,),
+        grid=(OWNERS // OWNER_BLOCK,),
         in_specs=[in_vmem] * 6,
-        out_specs=pl.BlockSpec((OWNERS, 2 * PAIRS, 128), lambda c: (0, c, 0)),
+        out_specs=pl.BlockSpec((OWNER_BLOCK, LIVE_DEV * 2 * PAIRS, 128), lambda step: (step, 0, 0)),
         out_shape=pltpu.HBM((OWNERS, LIVE_DEV * 2 * PAIRS, 128), bf16),
         scratch_shapes=[
             pltpu.VMEM((early_rows, half), bf16),
             pltpu.VMEM((early_rows, half), bf16),
             pltpu.VMEM((early_rows, 128), bf16),
             pltpu.VMEM((early_rows, 128), f32),
-            pltpu.VMEM((OWNERS * 2 * PAIRS, 128), f32),
+            pltpu.VMEM((LIVE_DEV, OWNERS * 2 * PAIRS, 128), f32),
         ],
         compiler_params=params,
         cost_estimate=cost(2e9, 14 * MIB),

time: 123 us -> 123 us (level)
  no operation moved by 1% of the time
where the time goes in v5:
time: 123 us; the launch traced here: 122 us
  blocking collectives  89.8 us (73%)
  Pallas kernels  25.6 us (21%)
  starting transfers between devices  4.59 us (4%)
  local copies, waits for them, and re-layouts  2.21 us (2%)
    all_to_all x1, blocking collectives, local(): lax.all_to_all(sent, ('feed', 'tm'), split_axis=0, concat_axis=0, tiled=T...  89.8 us
    pallas_call x1, Pallas kernels, local(): pl.pallas_call(beam_kernel, name='beams_and_power', in_specs=[in_vmem] *...  11.8 us
    pallas_call x1, Pallas kernels, local(): pl.pallas_call(spectra_kernel, name='spectra', grid=(OWNERS // OWNER_BLOC...  4.84 us
    ppermute x1, starting transfers between devices, local(): halo = lax.ppermute(history, 'tm', [(i, i + 1) for i in range(N_TM - 1)])  4.59 us
    pallas_call x1, Pallas kernels, local(): pl.pallas_call(late_spectra_kernel, name='late_spectra', in_specs=[in_vme...  3.64 us
    pallas_call x1, Pallas kernels, local(): pl.pallas_call(table_kernel, name='channel_table', out_shape=[jax.ShapeDt...  2.85 us
  transfers between devices with their start and end apart: 1, of which 0 were waited for; matrix products, arithmetic and copies ran while one was open for 0% of the time, Pallas kernels for 7%

profile of v5, /device:TPU:1, one launch (start us, length us, event | category | flops | bytes accessed | tf_op | source)
XLA Modules:
  0.0 122.3 jit_solution(572357516810371300)
XLA Ops:
  0.0 1.2 slice.3
  1.2 4.6 %collective-permute-start = (bf16[64,6144]{1,0:T(8,128)(2,1)S(1)}, bf16[64,6144]{1,0:T(8,128)(2,1)S(1)}, u32[]{:S(2)}, u32[]{:S(2)}) collective-permute-start(bf16[64,6144]{1,0:T(8,128)(2,1)S(1)} %slice.3), channel_id=1, source_target_pairs={{0,1},{1,2},{2,3},{3,4},{4,5},{5,6},{6,7},{8,9},{9,10},{10,11},{11... | collective-permute-start | bytes 2359304 | tf_op jit(solution)/shard_map/ppermute | solution.py:269
  5.8 0.0 copy-start.2
  5.8 0.7 copy-done.2
  6.5 0.0 copy-start
  6.5 0.0 copy-start.1
  6.5 2.8 %channel_table.1 = (bf16[2,768,1024]{2,1,0:T(8,128)(2,1)S(1)}, bf16[768,128]{1,0:T(8,128)(2,1)S(1)}) custom-call(s32[8,128]{1,0:T(8,128)S(1)} %bitcast.1), custom_call_target="tpu_custom_call" | custom-call | flops 4000000000 | bytes 3145728 | tf_op jit(solution)/shard_map/channel_table/pallas_call | solution.py:276
  9.3 0.0 copy-done
  9.4 0.0 copy-done.1
  9.4 2.4 %filter.1 = (bf16[768,1024]{1,0:T(8,128)(2,1)S(1)}, bf16[768,1024]{1,0:T(8,128)(2,1)S(1)}, bf16[768,128]{1,0:T(8,128)(2,1)S(1)}) custom-call(bf16[64,32768]{1,0:T(8,128)(2,1)S(1)} %copy-done, f32[4,2048]{1,0:T(4,128)S(1)} %copy-done.1, bf16[2,768,1024]{2,1,0:T(8,128)(2,1)S(1)} %get-tuple-element.10._.table_ref), custom_call_target="tpu_custom_call" | custom-call | flops 4000000000 | bytes 7340032 | tf_op jit(solution)/shard_map/filter/pallas_call | solution.py:284
  11.8 3.6 %late_spectra.1.late_ref = f32[3,4096,128]{2,1,0:T(8,128)S(1)} custom-call(bf16[2,768,1024]{2,1,0:T(8,128)(2,1)S(1)} %get-tuple-element.10._.table_ref, bf16[768,128]{1,0:T(8,128)(2,1)S(1)} %get-tuple-element.11.sign_ref, bf16[768,1024]{1,0:T(8,128)(2,1)S(1)} %get-tuple-element.12.even_ref, bf16[768,1024]{1,0:T(8,128)(2,1)S(1)} %get-tuple-element.13.odd_ref, ...), custom_call_target="tpu_custom_call" | custom-call | flops 4000000000 | bytes 12582912 | tf_op jit(solution)/shard_map/late_spectra/pallas_call | solution.py:297
  15.4 0.0 collective-permute-done.halo_ref
  15.5 4.8 %spectra.1 = bf16[256,48,128]{2,1,0:T(8,128)(2,1)} custom-call(bf16[64,6144]{1,0:T(8,128)(2,1)S(1)} %collective-permute-done.halo_ref, bf16[64,32768]{1,0:T(8,128)(2,1)S(1)} %copy-done, f32[4,2048]{1,0:T(4,128)S(1)} %copy-done.1, bf16[2,768,1024]{2,1,0:T(8,128)(2,1)S(1)} %get-tuple-element.10._.table_ref, bf16[768,128]{1,0:T(8,128)(2,1)S(1)} %get-tuple-element.11.sign_ref, ...), custom_call_target="tpu_custom_call" | custom-call | flops 2000000000 | bytes 14680064 | tf_op jit(solution)/shard_map/spectra/pallas_call | solution.py:306
  20.3 0.0 copy-start.5
  20.3 0.0 copy-start.3
  20.3 0.0 copy-start.4
  20.3 89.8 %all_to_all.5.recv_ref = bf16[256,48,128]{2,1,0:T(8,128)(2,1)S(1)} all-to-all(bf16[256,48,128]{2,1,0:T(8,128)(2,1)} %spectra.1), channel_id=1, replica_groups=mesh['feed'=32,'tm'=8] {'feed','tm'}, dimensions={0} | all-to-all | bytes 6291456 | tf_op jit(solution)/shard_map/all_to_all | solution.py:323
  110.1 0.0 copy-done.5
  110.2 0.3 broadcast_in_dim.2.slot_ref
  110.5 0.0 copy-done.3
  110.5 0.0 copy-done.4
  110.5 11.8 %beams_and_power.1 = f32[3,16,1024]{2,1,0:T(8,128)} custom-call(bf16[256,48,128]{2,1,0:T(8,128)(2,1)S(1)} %all_to_all.5.recv_ref, s32[2048,128]{1,0:T(8,128)S(1)} %broadcast_in_dim.2.slot_ref, bf16[512,512]{1,0:T(8,128)(2,1)S(1)} %copy-done.3, bf16[256,256]{1,0:T(8,128)(2,1)S(1)} %copy-done.4), custom_call_target="tpu_custom_call" | custom-call | flops 8999999488 | bytes 6291456 | tf_op jit(solution)/shard_map/beams_and_power/pallas_call | solution.py:326
Async XLA Ops:
  1.2 14.3 %collective-permute-start = (bf16[64,6144]{1,0:T(8,128)(2,1)S(1)}, bf16[64,6144]{1,0:T(8,128)(2,1)S(1)}, u32[]{:S(2)}, u32[]{:S(2)}) collective-permute-start(bf16[64,6144]{1,0:T(8,128)(2,1)S(1)} %slice.3), channel_id=1, source_target_pairs={{0,1},{1,2},{2,3},{3,4},{4,5},{5,6},{6,7},{8,9},{9,10},{10,11},{11... | collective-permute-start | bytes 2359304 | tf_op jit(solution)/shard_map/ppermute | solution.py:269
  5.8 0.7 copy-start.2
  6.5 2.9 %copy-start = (bf16[64,32768]{1,0:T(8,128)(2,1)S(1)}, bf16[64,32768]{1,0:T(8,128)(2,1)}, u32[]{:S(2)}) copy-start(bf16[64,32768]{1,0:T(8,128)(2,1)} %volt_ref.3) | copy-start | bytes 12582916
  6.5 2.9 %copy-start.1 = (f32[4,2048]{1,0:T(4,128)S(1)}, f32[4,2048]{1,0:T(4,128)}, u32[]{:S(2)}) copy-start(f32[4,2048]{1,0:T(4,128)} %constant.6.clone.window_ref) | copy-start | bytes 98308
  20.3 89.8 %copy-start.5 = (s32[2048]{0:T(1024)S(1)}, s32[2048]{0:T(1024)}, u32[]{:S(2)}) copy-start(s32[2048]{0:T(1024)} %param.7) | copy-start | bytes 24580
  20.3 90.2 %copy-start.3 = (bf16[512,512]{1,0:T(8,128)(2,1)S(1)}, bf16[512,512]{1,0:T(8,128)(2,1)}, u32[]{:S(2)}) copy-start(bf16[512,512]{1,0:T(8,128)(2,1)} %constant.7.clone.position_ref) | copy-start | bytes 1572868
  20.3 90.2 %copy-start.4 = (bf16[256,256]{1,0:T(8,128)(2,1)S(1)}, bf16[256,256]{1,0:T(8,128)(2,1)}, u32[]{:S(2)}) copy-start(bf16[256,256]{1,0:T(8,128)(2,1)} %constant.8.clone.sub_ref) | copy-start | bytes 393220

commit v6 on v5

--- a/solution.py
+++ b/solution.py
@@ -223,11 +223,11 @@
         return carry
 
     lax.fori_loop(0, N_FEED // 2, pairs, 0)
-    slot = jnp.concatenate([slot_ref[...]] * 2, axis=1)
+    slot = slot_ref[...]
     for i in range(groups):
-        want = lax.broadcasted_iota(jnp.int32, slot.shape, 1) + i * NS
+        want = lax.broadcasted_iota(jnp.int32, (NS, N_FEED * IN_DEV), 0) + i * NS
         place_ref[i % 2] = (slot == want).astype(jnp.float32).astype(jnp.bfloat16)
-        cells = jnp.dot(x_ref[...], place_ref[i % 2], preferred_element_type=jnp.float32)
+        cells = transposed_dot(x_ref[...], place_ref[i % 2])
         cells = cells.reshape(-1, 2, PAIRS, NS)
         both = [cells[:, r].reshape(-1, NS) for r in range(2)]
         cell_ref[i] = jnp.concatenate(both, axis=1).astype(jnp.bfloat16)
@@ -331,7 +331,7 @@
         out_shape=jax.ShapeDtypeStruct((LIVE_DEV, UPCH, CYL * NS), f32),
         scratch_shapes=[
             pltpu.VMEM((rows, inputs), bf16),
-            pltpu.VMEM((2, inputs, NS), bf16),
+            pltpu.VMEM((2, NS, inputs), bf16),
             pltpu.VMEM((2 * CYL, rows // 2, 2 * NS), bf16),
             pltpu.VMEM((2 * CYL, rows // 2, 2 * NS), f32),
             pltpu.VMEM((2, rows, CYL * NS), bf16),
@@ -340,7 +340,7 @@
         cost_estimate=cost(9e9, 6 * MIB),
     )(
         got,
-        jnp.broadcast_to(feed_slot[:, None], (inputs, 128)),
+        feed_slot.reshape(1, inputs),
         jnp.asarray(position_table(), dtype=bf16),
         jnp.asarray(sub_channel_table(), dtype=bf16),
     )

time: 123 us -> 122 us (level)
  no operation moved by 1% of the time
where the time goes in v6:
time: 122 us
  blocking collectives  89.8 us (74%)
  Pallas kernels  25.6 us (21%)
  starting transfers between devices  4.59 us (4%)
  local copies, waits for them, and re-layouts  1.88 us (2%)
    all_to_all x1, blocking collectives, local(): lax.all_to_all(sent, ('feed', 'tm'), split_axis=0, concat_axis=0, tiled=T...  89.8 us
    pallas_call x1, Pallas kernels, local(): pl.pallas_call(beam_kernel, name='beams_and_power', in_specs=[in_vmem] *...  11.9 us
    pallas_call x1, Pallas kernels, local(): pl.pallas_call(spectra_kernel, name='spectra', grid=(OWNERS // OWNER_BLOC...  4.84 us
    ppermute x1, starting transfers between devices, local(): halo = lax.ppermute(history, 'tm', [(i, i + 1) for i in range(N_TM - 1)])  4.59 us
    pallas_call x1, Pallas kernels, local(): pl.pallas_call(late_spectra_kernel, name='late_spectra', in_specs=[in_vme...  3.64 us
    pallas_call x1, Pallas kernels, local(): pl.pallas_call(table_kernel, name='channel_table', out_shape=[jax.ShapeDt...  2.85 us
  transfers between devices with their start and end apart: 1, of which 0 were waited for; matrix products, arithmetic and copies ran while one was open for 0% of the time, Pallas kernels for 7%

profile of v6, /device:TPU:1, one launch (start us, length us, event | category | flops | bytes accessed | tf_op | source)
XLA Modules:
  0.0 122.0 jit_solution(1279541829140369149)
XLA Ops:
  0.0 1.2 slice.3
  1.2 4.6 %collective-permute-start = (bf16[64,6144]{1,0:T(8,128)(2,1)S(1)}, bf16[64,6144]{1,0:T(8,128)(2,1)S(1)}, u32[]{:S(2)}, u32[]{:S(2)}) collective-permute-start(bf16[64,6144]{1,0:T(8,128)(2,1)S(1)} %slice.3), channel_id=1, source_target_pairs={{0,1},{1,2},{2,3},{3,4},{4,5},{5,6},{6,7},{8,9},{9,10},{10,11},{11... | collective-permute-start | bytes 2359304 | tf_op jit(solution)/shard_map/ppermute | solution.py:269
  5.8 0.0 copy-start.3
  5.8 0.7 copy-done.3
  6.5 0.0 copy-start
  6.5 0.0 copy-start.1
  6.5 2.8 %channel_table.1 = (bf16[2,768,1024]{2,1,0:T(8,128)(2,1)S(1)}, bf16[768,128]{1,0:T(8,128)(2,1)S(1)}) custom-call(s32[8,128]{1,0:T(8,128)S(1)} %bitcast.3), custom_call_target="tpu_custom_call" | custom-call | flops 4000000000 | bytes 3145728 | tf_op jit(solution)/shard_map/channel_table/pallas_call | solution.py:276
  9.3 0.0 copy-done
  9.4 0.0 copy-done.1
  9.4 2.4 %filter.1 = (bf16[768,1024]{1,0:T(8,128)(2,1)S(1)}, bf16[768,1024]{1,0:T(8,128)(2,1)S(1)}, bf16[768,128]{1,0:T(8,128)(2,1)S(1)}) custom-call(bf16[64,32768]{1,0:T(8,128)(2,1)S(1)} %copy-done, f32[4,2048]{1,0:T(4,128)S(1)} %copy-done.1, bf16[2,768,1024]{2,1,0:T(8,128)(2,1)S(1)} %get-tuple-element.10._.table_ref), custom_call_target="tpu_custom_call" | custom-call | flops 4000000000 | bytes 7340032 | tf_op jit(solution)/shard_map/filter/pallas_call | solution.py:284
  11.8 3.6 %late_spectra.1.late_ref = f32[3,4096,128]{2,1,0:T(8,128)S(1)} custom-call(bf16[2,768,1024]{2,1,0:T(8,128)(2,1)S(1)} %get-tuple-element.10._.table_ref, bf16[768,128]{1,0:T(8,128)(2,1)S(1)} %get-tuple-element.11.sign_ref, bf16[768,1024]{1,0:T(8,128)(2,1)S(1)} %get-tuple-element.12.even_ref, bf16[768,1024]{1,0:T(8,128)(2,1)S(1)} %get-tuple-element.13.odd_ref, ...), custom_call_target="tpu_custom_call" | custom-call | flops 4000000000 | bytes 12582912 | tf_op jit(solution)/shard_map/late_spectra/pallas_call | solution.py:297
  15.4 0.0 collective-permute-done.halo_ref
  15.5 4.8 %spectra.1 = bf16[256,48,128]{2,1,0:T(8,128)(2,1)} custom-call(bf16[64,6144]{1,0:T(8,128)(2,1)S(1)} %collective-permute-done.halo_ref, bf16[64,32768]{1,0:T(8,128)(2,1)S(1)} %copy-done, f32[4,2048]{1,0:T(4,128)S(1)} %copy-done.1, bf16[2,768,1024]{2,1,0:T(8,128)(2,1)S(1)} %get-tuple-element.10._.table_ref, bf16[768,128]{1,0:T(8,128)(2,1)S(1)} %get-tuple-element.11.sign_ref, ...), custom_call_target="tpu_custom_call" | custom-call | flops 2000000000 | bytes 14680064 | tf_op jit(solution)/shard_map/spectra/pallas_call | solution.py:306
  20.3 0.0 copy-start.2
  20.3 0.0 copy-start.4
  20.3 0.0 copy-start.5
  20.3 89.8 %all_to_all.5.recv_ref = bf16[256,48,128]{2,1,0:T(8,128)(2,1)S(1)} all-to-all(bf16[256,48,128]{2,1,0:T(8,128)(2,1)} %spectra.1), channel_id=1, replica_groups=mesh['feed'=32,'tm'=8] {'feed','tm'}, dimensions={0} | all-to-all | bytes 6291456 | tf_op jit(solution)/shard_map/all_to_all | solution.py:323
  110.1 0.0 copy-done.2
  110.2 0.0 copy-done.4
  110.2 0.0 copy-done.5
  110.2 11.9 %beams_and_power.1 = f32[3,16,1024]{2,1,0:T(8,128)} custom-call(bf16[256,48,128]{2,1,0:T(8,128)(2,1)S(1)} %all_to_all.5.recv_ref, s32[1,2048]{1,0:T(1,128)S(1)} %bitcast.2, bf16[512,512]{1,0:T(8,128)(2,1)S(1)} %copy-done.4, bf16[256,256]{1,0:T(8,128)(2,1)S(1)} %copy-done.5), custom_call_target="tpu_custom_call" | custom-call | flops 8999999488 | bytes 6291456 | tf_op jit(solution)/shard_map/beams_and_power/pallas_call | solution.py:326
Async XLA Ops:
  1.2 14.3 %collective-permute-start = (bf16[64,6144]{1,0:T(8,128)(2,1)S(1)}, bf16[64,6144]{1,0:T(8,128)(2,1)S(1)}, u32[]{:S(2)}, u32[]{:S(2)}) collective-permute-start(bf16[64,6144]{1,0:T(8,128)(2,1)S(1)} %slice.3), channel_id=1, source_target_pairs={{0,1},{1,2},{2,3},{3,4},{4,5},{5,6},{6,7},{8,9},{9,10},{10,11},{11... | collective-permute-start | bytes 2359304 | tf_op jit(solution)/shard_map/ppermute | solution.py:269
  5.8 0.7 copy-start.3
  6.5 2.9 %copy-start = (bf16[64,32768]{1,0:T(8,128)(2,1)S(1)}, bf16[64,32768]{1,0:T(8,128)(2,1)}, u32[]{:S(2)}) copy-start(bf16[64,32768]{1,0:T(8,128)(2,1)} %volt_ref.3) | copy-start | bytes 12582916
  6.5 2.9 %copy-start.1 = (f32[4,2048]{1,0:T(4,128)S(1)}, f32[4,2048]{1,0:T(4,128)}, u32[]{:S(2)}) copy-start(f32[4,2048]{1,0:T(4,128)} %constant.6.clone.window_ref) | copy-start | bytes 98308
  20.3 89.8 %copy-start.2 = (s32[2048]{0:T(1024)S(1)}, s32[2048]{0:T(1024)}, u32[]{:S(2)}) copy-start(s32[2048]{0:T(1024)} %param.7) | copy-start | bytes 24580
  20.3 89.8 %copy-start.4 = (bf16[512,512]{1,0:T(8,128)(2,1)S(1)}, bf16[512,512]{1,0:T(8,128)(2,1)}, u32[]{:S(2)}) copy-start(bf16[512,512]{1,0:T(8,128)(2,1)} %constant.7.clone.position_ref) | copy-start | bytes 1572868
  20.3 89.8 %copy-start.5 = (bf16[256,256]{1,0:T(8,128)(2,1)S(1)}, bf16[256,256]{1,0:T(8,128)(2,1)}, u32[]{:S(2)}) copy-start(bf16[256,256]{1,0:T(8,128)(2,1)} %constant.8.clone.sub_ref) | copy-start | bytes 393220

commit v7 on v6

--- a/solution.py
+++ b/solution.py
@@ -213,12 +213,12 @@
         for c in range(LIVE_DEV):
             for b in range(N_TM):
                 part = slice(c * 2 * PAIRS, (c + 1) * 2 * PAIRS)
-                one = recv_ref[2 * s * N_TM + b, part].astype(jnp.float32)
-                two = recv_ref[(2 * s + 1) * N_TM + b, part].astype(jnp.float32)
+                one = recv_ref[2 * s * N_TM + b, part]
+                two = recv_ref[(2 * s + 1) * N_TM + b, part]
                 even = jnp.where(low, one, two)
-                odd = pltpu.roll(jnp.where(low, two, one), 64, 1)
+                odd = pltpu.roll(jnp.where(low, two, one).astype(jnp.float32), 64, 1)
                 row = c * 256 + b * 32
-                x_ref[row : row + 16, pl.ds(lane, 128)] = even.astype(jnp.bfloat16)
+                x_ref[row : row + 16, pl.ds(lane, 128)] = even
                 x_ref[row + 16 : row + 32, pl.ds(lane, 128)] = odd.astype(jnp.bfloat16)
         return carry
 

time: 122 us -> 122 us (level)
  no operation moved by 1% of the time
where the time goes in v7:
time: 122 us
  blocking collectives  89.8 us (74%)
  Pallas kernels  25.6 us (21%)
  starting transfers between devices  4.59 us (4%)
  local copies, waits for them, and re-layouts  1.88 us (2%)
    all_to_all x1, blocking collectives, local(): lax.all_to_all(sent, ('feed', 'tm'), split_axis=0, concat_axis=0, tiled=T...  89.8 us
    pallas_call x1, Pallas kernels, local(): pl.pallas_call(beam_kernel, name='beams_and_power', in_specs=[in_vmem] *...  11.8 us
    pallas_call x1, Pallas kernels, local(): pl.pallas_call(spectra_kernel, name='spectra', grid=(OWNERS // OWNER_BLOC...  4.84 us
    ppermute x1, starting transfers between devices, local(): halo = lax.ppermute(history, 'tm', [(i, i + 1) for i in range(N_TM - 1)])  4.59 us
    pallas_call x1, Pallas kernels, local(): pl.pallas_call(late_spectra_kernel, name='late_spectra', in_specs=[in_vme...  3.64 us
    pallas_call x1, Pallas kernels, local(): pl.pallas_call(table_kernel, name='channel_table', out_shape=[jax.ShapeDt...  2.85 us
  transfers between devices with their start and end apart: 1, of which 0 were waited for; matrix products, arithmetic and copies ran while one was open for 0% of the time, Pallas kernels for 7%

profile of v7, /device:TPU:1, one launch (start us, length us, event | category | flops | bytes accessed | tf_op | source)
XLA Modules:
  0.0 121.9 jit_solution(11781405317710203145)
XLA Ops:
  0.0 1.2 slice.3
  1.2 4.6 %collective-permute-start = (bf16[64,6144]{1,0:T(8,128)(2,1)S(1)}, bf16[64,6144]{1,0:T(8,128)(2,1)S(1)}, u32[]{:S(2)}, u32[]{:S(2)}) collective-permute-start(bf16[64,6144]{1,0:T(8,128)(2,1)S(1)} %slice.3), channel_id=1, source_target_pairs={{0,1},{1,2},{2,3},{3,4},{4,5},{5,6},{6,7},{8,9},{9,10},{10,11},{11... | collective-permute-start | bytes 2359304 | tf_op jit(solution)/shard_map/ppermute | solution.py:269
  5.8 0.0 copy-start.3
  5.8 0.7 copy-done.3
  6.5 0.0 copy-start
  6.5 0.0 copy-start.1
  6.5 2.8 %channel_table.1 = (bf16[2,768,1024]{2,1,0:T(8,128)(2,1)S(1)}, bf16[768,128]{1,0:T(8,128)(2,1)S(1)}) custom-call(s32[8,128]{1,0:T(8,128)S(1)} %bitcast.3), custom_call_target="tpu_custom_call" | custom-call | flops 4000000000 | bytes 3145728 | tf_op jit(solution)/shard_map/channel_table/pallas_call | solution.py:276
  9.3 0.0 copy-done
  9.4 0.0 copy-done.1
  9.4 2.4 %filter.1 = (bf16[768,1024]{1,0:T(8,128)(2,1)S(1)}, bf16[768,1024]{1,0:T(8,128)(2,1)S(1)}, bf16[768,128]{1,0:T(8,128)(2,1)S(1)}) custom-call(bf16[64,32768]{1,0:T(8,128)(2,1)S(1)} %copy-done, f32[4,2048]{1,0:T(4,128)S(1)} %copy-done.1, bf16[2,768,1024]{2,1,0:T(8,128)(2,1)S(1)} %get-tuple-element.10._.table_ref), custom_call_target="tpu_custom_call" | custom-call | flops 4000000000 | bytes 7340032 | tf_op jit(solution)/shard_map/filter/pallas_call | solution.py:284
  11.8 3.6 %late_spectra.1.late_ref = f32[3,4096,128]{2,1,0:T(8,128)S(1)} custom-call(bf16[2,768,1024]{2,1,0:T(8,128)(2,1)S(1)} %get-tuple-element.10._.table_ref, bf16[768,128]{1,0:T(8,128)(2,1)S(1)} %get-tuple-element.11.sign_ref, bf16[768,1024]{1,0:T(8,128)(2,1)S(1)} %get-tuple-element.12.even_ref, bf16[768,1024]{1,0:T(8,128)(2,1)S(1)} %get-tuple-element.13.odd_ref, ...), custom_call_target="tpu_custom_call" | custom-call | flops 4000000000 | bytes 12582912 | tf_op jit(solution)/shard_map/late_spectra/pallas_call | solution.py:297
  15.4 0.0 collective-permute-done.halo_ref
  15.5 4.8 %spectra.1 = bf16[256,48,128]{2,1,0:T(8,128)(2,1)} custom-call(bf16[64,6144]{1,0:T(8,128)(2,1)S(1)} %collective-permute-done.halo_ref, bf16[64,32768]{1,0:T(8,128)(2,1)S(1)} %copy-done, f32[4,2048]{1,0:T(4,128)S(1)} %copy-done.1, bf16[2,768,1024]{2,1,0:T(8,128)(2,1)S(1)} %get-tuple-element.10._.table_ref, bf16[768,128]{1,0:T(8,128)(2,1)S(1)} %get-tuple-element.11.sign_ref, ...), custom_call_target="tpu_custom_call" | custom-call | flops 2000000000 | bytes 14680064 | tf_op jit(solution)/shard_map/spectra/pallas_call | solution.py:306
  20.3 0.0 copy-start.2
  20.3 0.0 copy-start.4
  20.3 0.0 copy-start.5
  20.3 89.8 %all_to_all.5.recv_ref = bf16[256,48,128]{2,1,0:T(8,128)(2,1)S(1)} all-to-all(bf16[256,48,128]{2,1,0:T(8,128)(2,1)} %spectra.1), channel_id=1, replica_groups=mesh['feed'=32,'tm'=8] {'feed','tm'}, dimensions={0} | all-to-all | bytes 6291456 | tf_op jit(solution)/shard_map/all_to_all | solution.py:323
  110.1 0.0 copy-done.2
  110.2 0.0 copy-done.4
  110.2 0.0 copy-done.5
  110.2 11.8 %beams_and_power.1 = f32[3,16,1024]{2,1,0:T(8,128)} custom-call(bf16[256,48,128]{2,1,0:T(8,128)(2,1)S(1)} %all_to_all.5.recv_ref, s32[1,2048]{1,0:T(1,128)S(1)} %bitcast.2, bf16[512,512]{1,0:T(8,128)(2,1)S(1)} %copy-done.4, bf16[256,256]{1,0:T(8,128)(2,1)S(1)} %copy-done.5), custom_call_target="tpu_custom_call" | custom-call | flops 8999999488 | bytes 6291456 | tf_op jit(solution)/shard_map/beams_and_power/pallas_call | solution.py:326
Async XLA Ops:
  1.2 14.3 %collective-permute-start = (bf16[64,6144]{1,0:T(8,128)(2,1)S(1)}, bf16[64,6144]{1,0:T(8,128)(2,1)S(1)}, u32[]{:S(2)}, u32[]{:S(2)}) collective-permute-start(bf16[64,6144]{1,0:T(8,128)(2,1)S(1)} %slice.3), channel_id=1, source_target_pairs={{0,1},{1,2},{2,3},{3,4},{4,5},{5,6},{6,7},{8,9},{9,10},{10,11},{11... | collective-permute-start | bytes 2359304 | tf_op jit(solution)/shard_map/ppermute | solution.py:269
  5.8 0.7 copy-start.3
  6.5 2.9 %copy-start = (bf16[64,32768]{1,0:T(8,128)(2,1)S(1)}, bf16[64,32768]{1,0:T(8,128)(2,1)}, u32[]{:S(2)}) copy-start(bf16[64,32768]{1,0:T(8,128)(2,1)} %volt_ref.3) | copy-start | bytes 12582916
  6.5 2.9 %copy-start.1 = (f32[4,2048]{1,0:T(4,128)S(1)}, f32[4,2048]{1,0:T(4,128)}, u32[]{:S(2)}) copy-start(f32[4,2048]{1,0:T(4,128)} %constant.6.clone.window_ref) | copy-start | bytes 98308
  20.3 89.8 %copy-start.2 = (s32[2048]{0:T(1024)S(1)}, s32[2048]{0:T(1024)}, u32[]{:S(2)}) copy-start(s32[2048]{0:T(1024)} %param.7) | copy-start | bytes 24580
  20.3 89.8 %copy-start.4 = (bf16[512,512]{1,0:T(8,128)(2,1)S(1)}, bf16[512,512]{1,0:T(8,128)(2,1)}, u32[]{:S(2)}) copy-start(bf16[512,512]{1,0:T(8,128)(2,1)} %constant.7.clone.position_ref) | copy-start | bytes 1572868
  20.3 89.8 %copy-start.5 = (bf16[256,256]{1,0:T(8,128)(2,1)S(1)}, bf16[256,256]{1,0:T(8,128)(2,1)}, u32[]{:S(2)}) copy-start(bf16[256,256]{1,0:T(8,128)(2,1)} %constant.8.clone.sub_ref) | copy-start | bytes 393220

commit v8 on v7

--- a/solution.py
+++ b/solution.py
@@ -216,10 +216,10 @@
                 one = recv_ref[2 * s * N_TM + b, part]
                 two = recv_ref[(2 * s + 1) * N_TM + b, part]
                 even = jnp.where(low, one, two)
-                odd = pltpu.roll(jnp.where(low, two, one).astype(jnp.float32), 64, 1)
+                odd = pltpu.roll(jnp.where(low, two, one), 64, 1)
                 row = c * 256 + b * 32
                 x_ref[row : row + 16, pl.ds(lane, 128)] = even
-                x_ref[row + 16 : row + 32, pl.ds(lane, 128)] = odd.astype(jnp.bfloat16)
+                x_ref[row + 16 : row + 32, pl.ds(lane, 128)] = odd
         return carry
 
     lax.fori_loop(0, N_FEED // 2, pairs, 0)

time: 122 us -> 122 us (level)
  no operation moved by 1% of the time
where the time goes in v8:
time: 122 us
  blocking collectives  89.8 us (74%)
  Pallas kernels  25.5 us (21%)
  starting transfers between devices  4.59 us (4%)
  local copies, waits for them, and re-layouts  1.88 us (2%)
    all_to_all x1, blocking collectives, local(): lax.all_to_all(sent, ('feed', 'tm'), split_axis=0, concat_axis=0, tiled=T...  89.8 us
    pallas_call x1, Pallas kernels, local(): pl.pallas_call(beam_kernel, name='beams_and_power', in_specs=[in_vmem] *...  11.7 us
    pallas_call x1, Pallas kernels, local(): pl.pallas_call(spectra_kernel, name='spectra', grid=(OWNERS // OWNER_BLOC...  4.84 us
    ppermute x1, starting transfers between devices, local(): halo = lax.ppermute(history, 'tm', [(i, i + 1) for i in range(N_TM - 1)])  4.59 us
    pallas_call x1, Pallas kernels, local(): pl.pallas_call(late_spectra_kernel, name='late_spectra', in_specs=[in_vme...  3.64 us
    pallas_call x1, Pallas kernels, local(): pl.pallas_call(table_kernel, name='channel_table', out_shape=[jax.ShapeDt...  2.85 us
  transfers between devices with their start and end apart: 1, of which 0 were waited for; matrix products, arithmetic and copies ran while one was open for 0% of the time, Pallas kernels for 7%

profile of v8, /device:TPU:1, one launch (start us, length us, event | category | flops | bytes accessed | tf_op | source)
XLA Modules:
  0.0 121.9 jit_solution(3365107238244328889)
XLA Ops:
  0.0 1.2 slice.3
  1.2 4.6 %collective-permute-start = (bf16[64,6144]{1,0:T(8,128)(2,1)S(1)}, bf16[64,6144]{1,0:T(8,128)(2,1)S(1)}, u32[]{:S(2)}, u32[]{:S(2)}) collective-permute-start(bf16[64,6144]{1,0:T(8,128)(2,1)S(1)} %slice.3), channel_id=1, source_target_pairs={{0,1},{1,2},{2,3},{3,4},{4,5},{5,6},{6,7},{8,9},{9,10},{10,11},{11... | collective-permute-start | bytes 2359304 | tf_op jit(solution)/shard_map/ppermute | solution.py:269
  5.8 0.0 copy-start.3
  5.8 0.7 copy-done.3
  6.5 0.0 copy-start
  6.5 0.0 copy-start.1
  6.5 2.8 %channel_table.1 = (bf16[2,768,1024]{2,1,0:T(8,128)(2,1)S(1)}, bf16[768,128]{1,0:T(8,128)(2,1)S(1)}) custom-call(s32[8,128]{1,0:T(8,128)S(1)} %bitcast.3), custom_call_target="tpu_custom_call" | custom-call | flops 4000000000 | bytes 3145728 | tf_op jit(solution)/shard_map/channel_table/pallas_call | solution.py:276
  9.3 0.0 copy-done
  9.4 0.0 copy-done.1
  9.4 2.4 %filter.1 = (bf16[768,1024]{1,0:T(8,128)(2,1)S(1)}, bf16[768,1024]{1,0:T(8,128)(2,1)S(1)}, bf16[768,128]{1,0:T(8,128)(2,1)S(1)}) custom-call(bf16[64,32768]{1,0:T(8,128)(2,1)S(1)} %copy-done, f32[4,2048]{1,0:T(4,128)S(1)} %copy-done.1, bf16[2,768,1024]{2,1,0:T(8,128)(2,1)S(1)} %get-tuple-element.10._.table_ref), custom_call_target="tpu_custom_call" | custom-call | flops 4000000000 | bytes 7340032 | tf_op jit(solution)/shard_map/filter/pallas_call | solution.py:284
  11.8 3.6 %late_spectra.1.late_ref = f32[3,4096,128]{2,1,0:T(8,128)S(1)} custom-call(bf16[2,768,1024]{2,1,0:T(8,128)(2,1)S(1)} %get-tuple-element.10._.table_ref, bf16[768,128]{1,0:T(8,128)(2,1)S(1)} %get-tuple-element.11.sign_ref, bf16[768,1024]{1,0:T(8,128)(2,1)S(1)} %get-tuple-element.12.even_ref, bf16[768,1024]{1,0:T(8,128)(2,1)S(1)} %get-tuple-element.13.odd_ref, ...), custom_call_target="tpu_custom_call" | custom-call | flops 4000000000 | bytes 12582912 | tf_op jit(solution)/shard_map/late_spectra/pallas_call | solution.py:297
  15.4 0.0 collective-permute-done.halo_ref
  15.5 4.8 %spectra.1 = bf16[256,48,128]{2,1,0:T(8,128)(2,1)} custom-call(bf16[64,6144]{1,0:T(8,128)(2,1)S(1)} %collective-permute-done.halo_ref, bf16[64,32768]{1,0:T(8,128)(2,1)S(1)} %copy-done, f32[4,2048]{1,0:T(4,128)S(1)} %copy-done.1, bf16[2,768,1024]{2,1,0:T(8,128)(2,1)S(1)} %get-tuple-element.10._.table_ref, bf16[768,128]{1,0:T(8,128)(2,1)S(1)} %get-tuple-element.11.sign_ref, ...), custom_call_target="tpu_custom_call" | custom-call | flops 2000000000 | bytes 14680064 | tf_op jit(solution)/shard_map/spectra/pallas_call | solution.py:306
  20.3 0.0 copy-start.2
  20.3 0.0 copy-start.4
  20.3 0.0 copy-start.5
  20.3 89.8 %all_to_all.5.recv_ref = bf16[256,48,128]{2,1,0:T(8,128)(2,1)S(1)} all-to-all(bf16[256,48,128]{2,1,0:T(8,128)(2,1)} %spectra.1), channel_id=1, replica_groups=mesh['feed'=32,'tm'=8] {'feed','tm'}, dimensions={0} | all-to-all | bytes 6291456 | tf_op jit(solution)/shard_map/all_to_all | solution.py:323
  110.1 0.0 copy-done.2
  110.2 0.0 copy-done.4
  110.2 0.0 copy-done.5
  110.2 11.7 %beams_and_power.1 = f32[3,16,1024]{2,1,0:T(8,128)} custom-call(bf16[256,48,128]{2,1,0:T(8,128)(2,1)S(1)} %all_to_all.5.recv_ref, s32[1,2048]{1,0:T(1,128)S(1)} %bitcast.2, bf16[512,512]{1,0:T(8,128)(2,1)S(1)} %copy-done.4, bf16[256,256]{1,0:T(8,128)(2,1)S(1)} %copy-done.5), custom_call_target="tpu_custom_call" | custom-call | flops 8999999488 | bytes 6291456 | tf_op jit(solution)/shard_map/beams_and_power/pallas_call | solution.py:326
Async XLA Ops:
  1.2 14.3 %collective-permute-start = (bf16[64,6144]{1,0:T(8,128)(2,1)S(1)}, bf16[64,6144]{1,0:T(8,128)(2,1)S(1)}, u32[]{:S(2)}, u32[]{:S(2)}) collective-permute-start(bf16[64,6144]{1,0:T(8,128)(2,1)S(1)} %slice.3), channel_id=1, source_target_pairs={{0,1},{1,2},{2,3},{3,4},{4,5},{5,6},{6,7},{8,9},{9,10},{10,11},{11... | collective-permute-start | bytes 2359304 | tf_op jit(solution)/shard_map/ppermute | solution.py:269
  5.8 0.7 copy-start.3
  6.5 2.9 %copy-start = (bf16[64,32768]{1,0:T(8,128)(2,1)S(1)}, bf16[64,32768]{1,0:T(8,128)(2,1)}, u32[]{:S(2)}) copy-start(bf16[64,32768]{1,0:T(8,128)(2,1)} %volt_ref.3) | copy-start | bytes 12582916
  6.5 2.9 %copy-start.1 = (f32[4,2048]{1,0:T(4,128)S(1)}, f32[4,2048]{1,0:T(4,128)}, u32[]{:S(2)}) copy-start(f32[4,2048]{1,0:T(4,128)} %constant.6.clone.window_ref) | copy-start | bytes 98308
  20.3 89.8 %copy-start.2 = (s32[2048]{0:T(1024)S(1)}, s32[2048]{0:T(1024)}, u32[]{:S(2)}) copy-start(s32[2048]{0:T(1024)} %param.7) | copy-start | bytes 24580
  20.3 89.8 %copy-start.4 = (bf16[512,512]{1,0:T(8,128)(2,1)S(1)}, bf16[512,512]{1,0:T(8,128)(2,1)}, u32[]{:S(2)}) copy-start(bf16[512,512]{1,0:T(8,128)(2,1)} %constant.7.clone.position_ref) | copy-start | bytes 1572868
  20.3 89.8 %copy-start.5 = (bf16[256,256]{1,0:T(8,128)(2,1)S(1)}, bf16[256,256]{1,0:T(8,128)(2,1)}, u32[]{:S(2)}) copy-start(bf16[256,256]{1,0:T(8,128)(2,1)} %constant.8.clone.sub_ref) | copy-start | bytes 393220
